TPU v7x, 128 devices: a whole 4x4x4 slice. The times are simulated.
128 devices in a mesh: seq: 16 (over z, x), tp: 2 (over core), dp: 4 (over y).
Axes of the slice: x: 4, y: 4, z: 4, core: 2. Of those that a mesh axis runs over, the one named last changes fastest.
Arguments:
- media_tokens: bfloat16 [4, 8192, 1408], P('dp', 'seq'), as said below
- latents: bfloat16 [1024, 1408], replicated, as said below
- query_weight: bfloat16 [1408, 1408], P(None, 'tp'), as said below
- key_weight: bfloat16 [1408, 1408], P(None, 'tp'), as said below
- value_weight: bfloat16 [1408, 1408], P(None, 'tp'), may hold values from -0.15625 to 0.15625
- out_weight: bfloat16 [1408, 1408], P('tp'), may hold values from -0.15625 to 0.15625
- cotangent: bfloat16 [4, 1024, 1408], P('dp'), may hold values from -6 to 6
Outputs:
- resampled: bfloat16 [4, 1024, 1408], P('dp', None, 'tp')
- grad_latents: float32 [1024, 1408], P('seq', ('tp', 'dp'))
- grad_query: float32 [1408, 1408], P(('seq', 'dp'), 'tp')
- grad_key: float32 [1408, 1408], P(('seq', 'dp'), 'tp')
- grad_value: float32 [1408, 1408], P(('seq', 'dp'), 'tp')
- grad_out: float32 [1408, 1408], P('tp', ('seq', 'dp'))
Inputs may be any that keep to these rules, and one draw needn't show every extreme that they name: `media_tokens`: video features of order one. `latents`: latent entries of order one. `query_weight`: entries of order 1408^-0.5. `key_weight`: entries of order 1408^-0.5.
All inputs are finite; a program needn't handle non-finite values.
Results may differ from a plain program's by a relative error of at most 0.034.
The roundings to bfloat16 on the way count: a program that leaves them out, or rounds other values in their place, can miss the bound.
Values sent between devices are 32-bit elements; how exact they have to be, the bound alone decides.
No kernel may reach another device: no remote copies, remote signals or barrier semaphores. Data moves between devices by JAX's collectives and lax.ppermute only.
A program may use at most 192 MiB of HBM per device.

v0:
```python
import jax
import jax.numpy as jnp
from jax import lax
from jax.sharding import PartitionSpec as P

HD = 88


def merged(part, axis, combine):
    gathered = jax.tree.map(lambda a: lax.all_gather(a, axis), part)

    def take(source):
        return jax.tree.map(lambda a: lax.dynamic_index_in_dim(a, source, 0, False), gathered)

    return lax.fori_loop(
        1, lax.axis_size(axis), lambda source, state: combine(state, take(source)), take(0)
    )


def layer_norm(rows):
    average = jnp.mean(rows, -1, keepdims=True)
    centered = rows - average
    variance = jnp.mean(centered * centered, -1, keepdims=True)
    inv_std = lax.rsqrt(variance + 1e-05)
    return (centered * inv_std, inv_std)


def norm_backward(normed, inv_std, upstream):
    mean_up = jnp.mean(upstream, -1, keepdims=True)
    mean_cross = jnp.mean(upstream * normed, -1, keepdims=True)
    return inv_std * (upstream - mean_up - normed * mean_cross)


def combine_softmax(first, second):
    top_max = jnp.maximum(first[0], second[0])
    left_factor = jnp.exp(first[0] - top_max)
    right_factor = jnp.exp(second[0] - top_max)
    total_sum = first[1] * left_factor + second[1] * right_factor
    total_weighted = first[2] * left_factor[..., None] + second[2] * right_factor[..., None]
    return (top_max, total_sum, total_weighted)


def local(media_tokens, latents, query_weight, key_weight, value_weight, out_weight, cotangent):
    width = query_weight.shape[1]
    head_count = width // HD
    latent_count = latents.shape[0]
    token_count = media_tokens.shape[1]
    block_rows = min(512, token_count)
    block_count = token_count // block_rows
    head_scale = HD ** (-0.5)
    contract_rows = (((0,), (0,)), ((), ()))
    contract_cols = (((1,), (1,)), ((), ()))
    latent_f = latents.astype(jnp.float32)
    latent_hat, latent_inv = layer_norm(latent_f)
    latent_norm = latent_hat.astype(jnp.bfloat16)
    queries = (
        jnp.dot(latent_norm, query_weight, preferred_element_type=jnp.float32) * head_scale
    ).astype(jnp.bfloat16)
    query_heads = queries.reshape(latent_count, head_count, HD).transpose(1, 0, 2)
    normed, unused_inv = layer_norm(media_tokens[0].astype(jnp.float32))
    media_norm = normed.astype(jnp.bfloat16)
    key_rows = jnp.dot(media_norm, key_weight, preferred_element_type=jnp.float32).astype(
        jnp.bfloat16
    )
    value_rows = jnp.dot(media_norm, value_weight, preferred_element_type=jnp.float32).astype(
        jnp.bfloat16
    )
    key_heads = key_rows.reshape(block_count, block_rows, head_count, HD).transpose(2, 0, 1, 3)
    value_heads = value_rows.reshape(block_count, block_rows, head_count, HD).transpose(2, 0, 1, 3)

    def head_forward(operands):
        query_head, key_blocks, value_blocks = operands

        def forward_step(state_now, blocks):
            row_max, row_sum, weighted = state_now
            key_block, value_block = blocks
            scores = lax.dot_general(
                query_head, key_block, contract_cols, preferred_element_type=jnp.float32
            )
            new_max = jnp.maximum(row_max, jnp.max(scores, -1))
            weights = jnp.exp(scores - new_max[:, None])
            factor = jnp.exp(row_max - new_max)
            row_sum = row_sum * factor + jnp.sum(weights, -1)
            weighted = weighted * factor[:, None] + jnp.dot(
                weights.astype(jnp.bfloat16), value_block, preferred_element_type=jnp.float32
            )
            return ((new_max, row_sum, weighted), None)

        initial = (
            jnp.full((latent_count,), -jnp.inf, jnp.float32),
            jnp.zeros((latent_count,), jnp.float32),
            jnp.zeros((latent_count, HD), jnp.float32),
        )
        final, unused_out = lax.scan(forward_step, initial, (key_blocks, value_blocks))
        return final

    local_max, local_sum, local_weighted = lax.map(
        head_forward, (query_heads, key_heads, value_heads)
    )
    row_max, row_sum, weighted = merged(
        (local_max, local_sum, local_weighted), "seq", combine_softmax
    )
    attended_heads = (weighted / row_sum[..., None]).astype(jnp.bfloat16)
    attended_flat = attended_heads.transpose(1, 0, 2).reshape(latent_count, width)
    partial_out = jnp.dot(attended_flat, out_weight, preferred_element_type=jnp.float32)
    summed = lax.psum_scatter(partial_out, "tp", scatter_dimension=1, tiled=True)
    column_count = summed.shape[1]
    latent_cols = lax.dynamic_slice_in_dim(
        latent_f, lax.axis_index("tp") * column_count, column_count, 1
    )
    resampled = (latent_cols + summed).astype(jnp.bfloat16)[None]
    upstream = cotangent[0]
    upstream_att = lax.dot_general(
        upstream, out_weight, contract_cols, preferred_element_type=jnp.float32
    ).astype(jnp.bfloat16)
    upstream_heads = upstream_att.reshape(latent_count, head_count, HD).transpose(1, 0, 2)
    row_delta = jnp.sum(upstream_heads.astype(jnp.float32) * attended_heads.astype(jnp.float32), -1)

    def head_backward(operands):
        query_head, key_blocks, value_blocks, upstream_head, head_max, head_sum, head_delta = (
            operands
        )

        def backward_step(query_total, blocks):
            key_block, value_block = blocks
            scores = lax.dot_general(
                query_head, key_block, contract_cols, preferred_element_type=jnp.float32
            )
            probs = jnp.exp(scores - head_max[:, None]) / head_sum[:, None]
            prob_grad = lax.dot_general(
                upstream_head, value_block, contract_cols, preferred_element_type=jnp.float32
            )
            score_grad = (probs * (prob_grad - head_delta[:, None])).astype(jnp.bfloat16)
            value_grad = lax.dot_general(
                probs.astype(jnp.bfloat16),
                upstream_head,
                contract_rows,
                preferred_element_type=jnp.float32,
            ).astype(jnp.bfloat16)
            key_grad = lax.dot_general(
                score_grad, query_head, contract_rows, preferred_element_type=jnp.float32
            ).astype(jnp.bfloat16)
            query_total = query_total + jnp.dot(
                score_grad, key_block, preferred_element_type=jnp.float32
            )
            return (query_total, (key_grad, value_grad))

        return lax.scan(
            backward_step, jnp.zeros((latent_count, HD), jnp.float32), (key_blocks, value_blocks)
        )

    query_total, (key_grads, value_grads) = lax.map(
        head_backward,
        (query_heads, key_heads, value_heads, upstream_heads, row_max, row_sum, row_delta),
    )
    key_grads = key_grads.transpose(1, 2, 0, 3).reshape(token_count, width)
    value_grads = value_grads.transpose(1, 2, 0, 3).reshape(token_count, width)
    key_term = lax.dot_general(
        media_norm, key_grads, contract_rows, preferred_element_type=jnp.float32
    )
    value_term = lax.dot_general(
        media_norm, value_grads, contract_rows, preferred_element_type=jnp.float32
    )
    query_flat = query_total.transpose(1, 0, 2).reshape(latent_count, width)
    query_block = lax.psum_scatter(query_flat, "seq", scatter_dimension=0, tiled=True)
    share_rows = query_block.shape[0]
    row_start = lax.axis_index("seq") * share_rows
    query_proj = (query_block * head_scale).astype(jnp.bfloat16)
    norm_block = lax.dynamic_slice_in_dim(latent_norm, row_start, share_rows, 0)
    query_term = lax.dot_general(
        norm_block, query_proj, contract_rows, preferred_element_type=jnp.float32
    )
    upstream_block = lax.dynamic_slice_in_dim(upstream, row_start, share_rows, 0)
    grad_query, grad_key, grad_value = (
        lax.psum_scatter(query_term, ("seq", "dp"), scatter_dimension=0, tiled=True),
        lax.psum_scatter(key_term, ("seq", "dp"), scatter_dimension=0, tiled=True),
        lax.psum_scatter(value_term, ("seq", "dp"), scatter_dimension=0, tiled=True),
    )
    attended_block = lax.dynamic_slice_in_dim(attended_flat, row_start, share_rows, 0)
    out_term = lax.dot_general(
        attended_block, upstream_block, contract_rows, preferred_element_type=jnp.float32
    )
    grad_out = lax.psum_scatter(out_term, ("seq", "dp"), scatter_dimension=1, tiled=True)
    latent_up = lax.dot_general(
        query_proj, query_weight, contract_cols, preferred_element_type=jnp.float32
    )
    hat_block = lax.dynamic_slice_in_dim(latent_hat, row_start, share_rows, 0)
    inv_block = lax.dynamic_slice_in_dim(latent_inv, row_start, share_rows, 0)
    latent_term = norm_backward(hat_block, inv_block, latent_up) + upstream_block.astype(
        jnp.float32
    ) / lax.axis_size("tp")
    grad_latents = lax.psum_scatter(latent_term, ("tp", "dp"), scatter_dimension=1, tiled=True)
    return (resampled, grad_latents, grad_query, grad_key, grad_value, grad_out)


def solution(mesh):
    placed = (
        P("dp", "seq", None),
        P(),
        P(None, "tp"),
        P(None, "tp"),
        P(None, "tp"),
        P("tp", None),
        P("dp", None, None),
    )
    return jax.shard_map(
        local,
        mesh=mesh,
        in_specs=placed,
        out_specs=(
            P("dp", None, "tp"),
            P("seq", ("tp", "dp")),
            P(("seq", "dp"), "tp"),
            P(("seq", "dp"), "tp"),
            P(("seq", "dp"), "tp"),
            P("tp", ("seq", "dp")),
        ),
        check_vma=False,
    )
```

profile of v0, /device:TPU:0, one launch (start us, length us, event | category | flops | bytes accessed | tf_op | source)
XLA Modules:
  0.0 1203.1 jit_solution(15464347647950295269)
XLA Ops:
  44.6 33.5 %while.40 = (s32[]{:T(128)}, f32[8,1024]{1,0:T(8,128)S(1)}, f32[8,1024]{1,0:T(8,128)S(1)}, f32[8,1024,88]{1,2,0:T(8,128)}, bf16[8,1024,88]{2,1,0:T(8,128)(2,1)},...) while((s32[]{:T(128)}, f32[8,1024]{1,0:T(8,128)S(1)}, ...), condition=%wide.region_7.8_spmd, body=%wide.region_4.7_spmd.sunk | while | flops 187264000 | bytes 7235685 | solution.py:97
  78.1 26.3 %all-gather = f32[128,1024]{1,0:T(8,128)S(1)} all-gather(f32[8,1024]{1,0:T(8,128)S(1)} %get-tuple-element.336), channel_id=2, replica_groups=mesh['seq'=16,'tp'=2,'dp'=4] {'seq'}, dimensions={0}, use_global_device_ids=true | all-gather | bytes 557056 | tf_op jit(solution)/shard_map/all_gather | solution.py:10
  104.4 24.5 %all-gather.1 = f32[128,1024]{1,0:T(8,128)S(1)} all-gather(f32[8,1024]{1,0:T(8,128)S(1)} %get-tuple-element.337), channel_id=3, replica_groups=mesh['seq'=16,'tp'=2,'dp'=4] {'seq'}, dimensions={0}, use_global_device_ids=true | all-gather | bytes 557056 | tf_op jit(solution)/shard_map/all_gather | solution.py:10
  135.0 210.6 %all-gather.5.cloned.1.call-done = f32[128,1024,88]{1,2,0:T(8,128)} async-done(((f32[8,1024,88]{1,2,0:T(8,128)}), f32[128,1024,88]{1,2,0:T(8,128)}) %all-gather.5.cloned.1.call-update) | async-done | bytes 46137360 | tf_op jit(solution)/shard_map/all_gather | solution.py:10
  354.2 259.3 %while.41 = (s32[]{:T(128)}, f32[8,1024]{1,0:T(8,128)S(1)}, f32[8,1024]{1,0:T(8,128)S(1)}, f32[8,1024,88]{2,1,0:T(8,128)}, f32[16,8,1024]{2,1,0:T(8,128)S(1)}, /...) while((s32[]{:T(128)}, f32[8,1024]{1,0:T(8,128)S(1)}, ...), condition=%wide.region_9.10_spmd, body=%wide.region_8.9_spmd.sunk | while | flops 2211845 | bytes 20512920 | solution.py:15
  363.6 7.9 fusion.121
  380.9 7.9 fusion.121
  398.2 7.9 fusion.121
  415.5 7.9 fusion.121
  432.7 7.9 fusion.121
  450.0 7.9 fusion.121
  467.3 7.9 fusion.121
  484.6 7.9 fusion.121
  501.9 7.9 fusion.121
  519.2 7.9 fusion.121
  536.4 7.9 fusion.121
  624.6 72.2 %while.42 = (s32[]{:T(128)}, f32[8,1024,88]{1,2,0:T(8,128)}, bf16[8,1,512,88]{2,3,1,0:T(8,128)(2,1)}, bf16[8,1,512,88]{2,3,1,0:T(8,128)(2,1)}, bf16[8,1024,88]{2...) while((s32[]{:T(128)}, f32[8,1024,88]{1,2,0:T(8,128)}, ...), condition=%wide.region_13.14_spmd, body=%wide.region_12.13_spmd.sunk | while | flops 464609280 | bytes 11297917 | solution.py:152
  701.3 74.5 %reduce-scatter.18.cloned.1.call-done = f32[64,704]{1,0:T(8,128)} async-done(((f32[1024,704]{1,0:T(8,128)}), f32[64,704]{1,0:T(8,128)}) %reduce-scatter.18.cloned.1.call-update) | async-done | bytes 180240
  809.7 250.2 %fusion.78 = (f32[24,704]{1,0:T(8,128)S(1)}, f32[24,704]{1,0:T(8,128)S(1)}, f32[24,704]{1,0:T(8,128)S(1)}, f32[704,24]{0,1:T(8,128)S(1)}) fusion(f32[1408,704]{1,0:T(8,128)} %fusion.62, f32[1408,704]{1,0:T(8,128)} %fusion.74, f32[1408,704]{1,0:T(8,128)} %fusion.72, f32[704,1408]{0,1:T(8,128)} %fusion.64), kind=kCustom, calls=%all-reduce-scatter.4 | all-reduce-scatter fusion | flops 4325377 | bytes 16130560
  1094.6 9.8 collective-permute-start.10
  1108.5 16.4 %collective-permute-start.7 = (f32[24,704]{1,0:T(8,128)S(1)}, f32[24,704]{1,0:T(8,128)S(1)}, u32[]{:S(2)}, u32[]{:S(2)}) collective-permute-start(f32[24,704]{1,0:T(8,128)S(1)} %get-tuple-element.447), channel_id=1, source_target_pairs={{0,2},{1,3},{2,8},{3,9},{8,10},{9,11},{10,16},{11,17},{16,18},{17,... | collective-permute-start | bytes 202760
  1155.9 10.4 concatenate.2
  1166.3 9.6 concatenate.1
  1175.9 9.6 concatenate
  (327 shorter events, 458.2 us)
Async XLA Ops:
  7.2 338.4 %all-gather.5.cloned.1.call-start = ((), (), s32[]{:S(2)}) async-start(), calls=%async_computation.5 | async-start | bytes 49020928 | tf_op jit(solution)/shard_map/all_gather | solution.py:10
  78.1 697.8 %reduce-scatter.18.cloned.1.call-start = ((), (), s32[]{:S(2)}) async-start(), calls=%async_computation.6 | async-start | bytes 3342336
  700.3 490.5 %reduce-scatter.16.cloned.1.call-start = ((), (), s32[]{:S(2)}) async-start(), calls=%async_computation.4 | async-start | bytes 811008 | tf_op jit(solution)/shard_map/reduce_scatter | solution.py:192
  786.2 406.2 %reduce-scatter.14.cloned.1.call-start = ((), (), s32[]{:S(2)}) async-start(), calls=%async_computation.3 | async-start | bytes 8650752 | tf_op jit(solution)/shard_map/reduce_scatter | solution.py:106
  1060.0 9.3 collective-permute-start.23
  1066.3 10.0 collective-permute-start.18
  1070.6 12.7 %collective-permute-start.20 = (f32[704,24]{0,1:T(8,128)S(1)}, f32[704,24]{0,1:T(8,128)S(1)}, u32[]{:S(2)}, u32[]{:S(2)}) collective-permute-start(f32[704,24]{0,1:T(8,128)S(1)} %get-tuple-element.449), channel_id=1, source_target_pairs={{0,3},{1,8},{2,9},{3,10},{8,11},{9,16},{10,17},{11,18},{16,19},{17... | collective-permute-start | bytes 202760
  1071.9 12.9 %collective-permute-start.21 = (f32[704,24]{0,1:T(8,128)S(1)}, f32[704,24]{0,1:T(8,128)S(1)}, u32[]{:S(2)}, u32[]{:S(2)}) collective-permute-start(f32[704,24]{0,1:T(8,128)S(1)} %get-tuple-element.449), channel_id=1, source_target_pairs={{0,8},{1,9},{2,10},{3,11},{8,16},{9,17},{10,18},{11,19},{16,24},{1... | collective-permute-start | bytes 202760
  1074.1 17.9 %collective-permute-start.22 = (f32[704,24]{0,1:T(8,128)S(1)}, f32[704,24]{0,1:T(8,128)S(1)}, u32[]{:S(2)}, u32[]{:S(2)}) collective-permute-start(f32[704,24]{0,1:T(8,128)S(1)} %get-tuple-element.449), channel_id=1, source_target_pairs={{0,9},{1,10},{2,11},{3,16},{8,17},{9,18},{10,19},{11,24},{16,25},{... | collective-permute-start | bytes 202760
  1076.3 18.2 %collective-permute-start.12 = (f32[24,704]{1,0:T(8,128)S(1)}, f32[24,704]{1,0:T(8,128)S(1)}, u32[]{:S(2)}, u32[]{:S(2)}) collective-permute-start(f32[24,704]{1,0:T(8,128)S(1)} %get-tuple-element.448), channel_id=1, source_target_pairs={{0,1},{1,2},{2,3},{3,8},{8,9},{9,10},{10,11},{11,16},{16,17},{17,1... | collective-permute-start | bytes 202760
  1078.2 26.2 %collective-permute-start.13 = (f32[24,704]{1,0:T(8,128)S(1)}, f32[24,704]{1,0:T(8,128)S(1)}, u32[]{:S(2)}, u32[]{:S(2)}) collective-permute-start(f32[24,704]{1,0:T(8,128)S(1)} %get-tuple-element.448), channel_id=1, source_target_pairs={{0,2},{1,3},{2,8},{3,9},{8,10},{9,11},{10,16},{11,17},{16,18},{17,... | collective-permute-start | bytes 202760
  1083.3 25.2 %collective-permute-start.14 = (f32[24,704]{1,0:T(8,128)S(1)}, f32[24,704]{1,0:T(8,128)S(1)}, u32[]{:S(2)}, u32[]{:S(2)}) collective-permute-start(f32[24,704]{1,0:T(8,128)S(1)} %get-tuple-element.448), channel_id=1, source_target_pairs={{0,3},{1,8},{2,9},{3,10},{8,11},{9,16},{10,17},{11,18},{16,19},{17... | collective-permute-start | bytes 202760
  1084.8 40.1 %collective-permute-start.15 = (f32[24,704]{1,0:T(8,128)S(1)}, f32[24,704]{1,0:T(8,128)S(1)}, u32[]{:S(2)}, u32[]{:S(2)}) collective-permute-start(f32[24,704]{1,0:T(8,128)S(1)} %get-tuple-element.448), channel_id=1, source_target_pairs={{0,8},{1,9},{2,10},{3,11},{8,16},{9,17},{10,18},{11,19},{16,24},{1... | collective-permute-start | bytes 202760
  1092.0 34.7 %collective-permute-start.16 = (f32[24,704]{1,0:T(8,128)S(1)}, f32[24,704]{1,0:T(8,128)S(1)}, u32[]{:S(2)}, u32[]{:S(2)}) collective-permute-start(f32[24,704]{1,0:T(8,128)S(1)} %get-tuple-element.448), channel_id=1, source_target_pairs={{0,9},{1,10},{2,11},{3,16},{8,17},{9,18},{10,19},{11,24},{16,25},{... | collective-permute-start | bytes 202760
  1094.6 34.7 %collective-permute-start.10 = (f32[24,704]{1,0:T(8,128)S(1)}, f32[24,704]{1,0:T(8,128)S(1)}, u32[]{:S(2)}, u32[]{:S(2)}) collective-permute-start(f32[24,704]{1,0:T(8,128)S(1)} %get-tuple-element.447), channel_id=1, source_target_pairs={{0,9},{1,10},{2,11},{3,16},{8,17},{9,18},{10,19},{11,24},{16,25},{... | collective-permute-start | bytes 202760
  1104.4 27.6 %collective-permute-start.6 = (f32[24,704]{1,0:T(8,128)S(1)}, f32[24,704]{1,0:T(8,128)S(1)}, u32[]{:S(2)}, u32[]{:S(2)}) collective-permute-start(f32[24,704]{1,0:T(8,128)S(1)} %get-tuple-element.447), channel_id=1, source_target_pairs={{0,1},{1,2},{2,3},{3,8},{8,9},{9,10},{10,11},{11,16},{16,17},{17,1... | collective-permute-start | bytes 202760
  1108.5 26.7 %collective-permute-start.7 = (f32[24,704]{1,0:T(8,128)S(1)}, f32[24,704]{1,0:T(8,128)S(1)}, u32[]{:S(2)}, u32[]{:S(2)}) collective-permute-start(f32[24,704]{1,0:T(8,128)S(1)} %get-tuple-element.447), channel_id=1, source_target_pairs={{0,2},{1,3},{2,8},{3,9},{8,10},{9,11},{10,16},{11,17},{16,18},{17,... | collective-permute-start | bytes 202760
  1124.9 14.0 %collective-permute-start.8 = (f32[24,704]{1,0:T(8,128)S(1)}, f32[24,704]{1,0:T(8,128)S(1)}, u32[]{:S(2)}, u32[]{:S(2)}) collective-permute-start(f32[24,704]{1,0:T(8,128)S(1)} %get-tuple-element.447), channel_id=1, source_target_pairs={{0,3},{1,8},{2,9},{3,10},{8,11},{9,16},{10,17},{11,18},{16,19},{17... | collective-permute-start | bytes 202760
  1126.7 14.2 %collective-permute-start.9 = (f32[24,704]{1,0:T(8,128)S(1)}, f32[24,704]{1,0:T(8,128)S(1)}, u32[]{:S(2)}, u32[]{:S(2)}) collective-permute-start(f32[24,704]{1,0:T(8,128)S(1)} %get-tuple-element.447), channel_id=1, source_target_pairs={{0,8},{1,9},{2,10},{3,11},{8,16},{9,17},{10,18},{11,19},{16,24},{1... | collective-permute-start | bytes 202760
  1129.3 46.6 %collective-permute-start = (f32[24,704]{1,0:T(8,128)S(1)}, f32[24,704]{1,0:T(8,128)}, u32[]{:S(2)}, u32[]{:S(2)}) collective-permute-start(f32[24,704]{1,0:T(8,128)S(1)} %get-tuple-element.446), channel_id=1, source_target_pairs={{0,1},{1,2},{2,3},{3,8},{8,9},{9,10},{10,11},{11,16},{16,17},{17,1... | collective-permute-start | bytes 202760
  1132.0 43.8 %collective-permute-start.1 = (f32[24,704]{1,0:T(8,128)S(1)}, f32[24,704]{1,0:T(8,128)}, u32[]{:S(2)}, u32[]{:S(2)}) collective-permute-start(f32[24,704]{1,0:T(8,128)S(1)} %get-tuple-element.446), channel_id=1, source_target_pairs={{0,2},{1,3},{2,8},{3,9},{8,10},{9,11},{10,16},{11,17},{16,18},{17,... | collective-permute-start | bytes 202760
  1135.2 40.7 %collective-permute-start.2 = (f32[24,704]{1,0:T(8,128)S(1)}, f32[24,704]{1,0:T(8,128)}, u32[]{:S(2)}, u32[]{:S(2)}) collective-permute-start(f32[24,704]{1,0:T(8,128)S(1)} %get-tuple-element.446), channel_id=1, source_target_pairs={{0,3},{1,8},{2,9},{3,10},{8,11},{9,16},{10,17},{11,18},{16,19},{17... | collective-permute-start | bytes 202760
  1139.0 36.9 %collective-permute-start.3 = (f32[24,704]{1,0:T(8,128)S(1)}, f32[24,704]{1,0:T(8,128)}, u32[]{:S(2)}, u32[]{:S(2)}) collective-permute-start(f32[24,704]{1,0:T(8,128)S(1)} %get-tuple-element.446), channel_id=1, source_target_pairs={{0,8},{1,9},{2,10},{3,11},{8,16},{9,17},{10,18},{11,19},{16,24},{1... | collective-permute-start | bytes 202760
  1140.9 35.0 %collective-permute-start.4 = (f32[24,704]{1,0:T(8,128)S(1)}, f32[24,704]{1,0:T(8,128)}, u32[]{:S(2)}, u32[]{:S(2)}) collective-permute-start(f32[24,704]{1,0:T(8,128)S(1)} %get-tuple-element.446), channel_id=1, source_target_pairs={{0,9},{1,10},{2,11},{3,16},{8,17},{9,18},{10,19},{11,24},{16,25},{... | collective-permute-start | bytes 202760
  (30 other events, 878.6 us)
Sparse Core Ops, SparseCore 0:
  78.2 267.3 all-gather.4
  700.4 75.4 reduce-scatter.17
  786.3 85.7 reduce-scatter.15
  874.4 121.2 reduce-scatter.13
where the time goes:
time: 1210 us; the launch traced here: 1200 us
  blocking collectives  301 us (25%)
  waiting for transfers between devices  285 us (24%)
  local copies, waits for them, and re-layouts  213 us (18%)
  other arithmetic  162 us (13%)
  matrix products  143 us (12%)
  starting transfers between devices  83.1 us (7%)
  between operations  15.1 us (1%)
    unnamed x1, blocking collectives  250 us
    all_gather x1, waiting for transfers between devices, merged(): gathered = jax.tree.map(lambda a: lax.all_gather(a, axis), part)  211 us
    dynamic_slice x33, local copies, waits for them, and re-layouts, take(): lax.dynamic_index_in_dim(a, source, 0, False)  132 us
    add x15, other arithmetic, combine_softmax(): first[2] * left_factor[..., None] + second[2] * right_factor[..., None]  119 us
    unnamed x25, starting transfers between devices  82.8 us
    unnamed x29, waiting for transfers between devices  74.6 us
    unnamed x69, local copies, waits for them, and re-layouts  53.8 us
    all_gather x2, blocking collectives, merged(): gathered = jax.tree.map(lambda a: lax.all_gather(a, axis), part)  50.8 us
  transfers between devices with their start and end apart: 28, of which 2 were waited for; matrix products, arithmetic and copies ran while one was open for 27% of the time, Pallas kernels for 0%

commit v1 on v0

v1 whole, which is shorter than its diff:
```python
import functools

import jax
import jax.numpy as jnp
from jax import lax
from jax.experimental import pallas as pl
from jax.experimental.pallas import tpu as pltpu
from jax.sharding import PartitionSpec as P

HD = 88
VMEM = 56 * 1024 * 1024
F32 = jnp.float32
BF16 = jnp.bfloat16
NT = (((1,), (1,)), ((), ()))
TN = (((0,), (0,)), ((), ()))


def params():
    return pltpu.CompilerParams(vmem_limit_bytes=VMEM)


def cost(flops, size):
    return pl.CostEstimate(flops=int(flops), bytes_accessed=int(size), transcendentals=0)


def dot(a, b, dims=(((1,), (0,)), ((), ()))):
    return lax.dot_general(a, b, dims, preferred_element_type=F32)


def layer_norm(rows):
    average = jnp.mean(rows, -1, keepdims=True)
    centered = rows - average
    variance = jnp.mean(centered * centered, -1, keepdims=True)
    inv_std = lax.rsqrt(variance + 1e-05)
    return (centered * inv_std, inv_std)


def norm_backward(normed, inv_std, upstream):
    mean_up = jnp.mean(upstream, -1, keepdims=True)
    mean_cross = jnp.mean(upstream * normed, -1, keepdims=True)
    return inv_std * (upstream - mean_up - normed * mean_cross)


def project_kernel(
    media_ref, latents_ref, cot_ref, qw_ref, kw_ref, vw_ref, ow_ref,
    mn_ref, ln_ref, q_ref, k_ref, v_ref, u_ref,
):
    def split(ref, value):
        for head in range(ref.shape[0]):
            ref[head] = value[head * HD : (head + 1) * HD, :].astype(BF16)

    media_norm = layer_norm(media_ref[...].astype(F32))[0].T.astype(BF16)
    mn_ref[...] = media_norm
    split(k_ref, dot(kw_ref[...], media_norm))
    split(v_ref, dot(vw_ref[...], media_norm))
    latent_norm = layer_norm(latents_ref[...].astype(F32))[0].T.astype(BF16)
    ln_ref[...] = latent_norm
    split(q_ref, dot(qw_ref[...], latent_norm) * HD ** (-0.5))
    split(u_ref, dot(ow_ref[...], cot_ref[...], NT))


def project(media, latents, cot, qw, kw, vw, ow):
    tokens, width = media.shape
    count = latents.shape[0]
    inner = qw.shape[0]
    heads = inner // HD
    steps = 2
    t, c = tokens // steps, count // steps
    rows = lambda n: pl.BlockSpec((n, width), lambda i: (i, 0))
    cols = lambda n: pl.BlockSpec((width, n), lambda i: (0, i))
    whole = lambda a: pl.BlockSpec(a.shape, lambda i: (0, 0))
    turned = lambda n: pl.BlockSpec((heads, HD, n), lambda i: (0, 0, i))
    shape = jax.ShapeDtypeStruct
    return pl.pallas_call(
        project_kernel,
        grid=(steps,),
        in_specs=[rows(t), rows(c), rows(c), whole(qw), whole(kw), whole(vw), whole(ow)],
        out_specs=[cols(t), cols(c), turned(c), turned(t), turned(t), turned(c)],
        out_shape=[
            shape((width, tokens), BF16),
            shape((width, count), BF16),
            shape((heads, HD, count), BF16),
            shape((heads, HD, tokens), BF16),
            shape((heads, HD, tokens), BF16),
            shape((heads, HD, count), BF16),
        ],
        compiler_params=params(),
        cost_estimate=cost(4 * (tokens + count) * width * inner, 24e6),
        name="project",
    )(media, latents, cot, qw, kw, vw, ow)


def forward_kernel(chunk, q_ref, k_ref, v_ref, u_ref, w_ref, stat_ref):
    head = pl.program_id(0)
    count = q_ref.shape[2]
    half = count // 2
    keys = k_ref[0].astype(F32).T.astype(BF16)
    vals = v_ref[0]
    for start in range(0, count, chunk):
        cols = slice(start, start + chunk)
        scores = dot(keys, q_ref[0, :, cols])
        top = jnp.max(scores, 0, keepdims=True)
        weights = jnp.exp(scores - top)
        total = jnp.sum(weights, 0, keepdims=True)
        weighted = dot(vals, weights.astype(BF16))
        delta = jnp.sum(u_ref[0, :, cols].astype(F32) * weighted, 0, keepdims=True)
        side, inner = divmod(start, half)
        w_ref[side, 0, :, inner : inner + chunk] = weighted
        stat_ref[0, pl.ds(head, 1), cols] = top
        stat_ref[1, pl.ds(head, 1), cols] = total
        stat_ref[2, pl.ds(head, 1), cols] = delta


def forward(q, k, v, u):
    heads, _, count = q.shape
    tokens = k.shape[2]
    per_head = lambda n: pl.BlockSpec((1, HD, n), lambda h: (h, 0, 0))
    return pl.pallas_call(
        functools.partial(forward_kernel, min(256, count // 2)),
        grid=(heads,),
        in_specs=[per_head(count), per_head(tokens), per_head(tokens), per_head(count)],
        out_specs=[
            pl.BlockSpec((2, 1, HD, count // 2), lambda h: (0, h, 0, 0)),
            pl.BlockSpec((3, heads, count), lambda h: (0, 0, 0)),
        ],
        out_shape=[
            jax.ShapeDtypeStruct((2, heads, HD, count // 2), F32),
            jax.ShapeDtypeStruct((3, heads, count), F32),
        ],
        compiler_params=params(),
        cost_estimate=cost(16 * heads * count * tokens * HD, 9e6),
        name="attend",
    )(q, k, v, u)


def backward_kernel(
    chunk, q_ref, k_ref, v_ref, u_ref, lse_ref, delta_ref, dq_ref, dk_ref, dv_ref, done_ref
):
    head = pl.program_id(0)
    count = q_ref.shape[2]
    half = count // 2
    keys_t = k_ref[0]
    keys = keys_t.astype(F32).T.astype(BF16)
    vals = v_ref[0].astype(F32).T.astype(BF16)
    key_grad = jnp.zeros(keys.shape, F32)
    value_grad = jnp.zeros(vals.shape, F32)
    for start in range(0, count, chunk):
        cols = slice(start, start + chunk)
        q = q_ref[0, :, cols]
        u = u_ref[0, :, cols]
        probs = jnp.exp(dot(keys, q) - lse_ref[pl.ds(head, 1), cols])
        grad = (probs * (dot(vals, u) - delta_ref[pl.ds(head, 1), cols])).astype(BF16)
        value_grad += dot(probs.astype(BF16), u.astype(F32).T.astype(BF16))
        key_grad += dot(grad, q.astype(F32).T.astype(BF16))
        side, inner = divmod(start, half)
        dq_ref[side, 0, :, inner : inner + chunk] = dot(keys_t, grad)
    dk_ref[0] = key_grad.T.astype(BF16)
    dv_ref[0] = value_grad.T.astype(BF16)
    done_ref[...] = jnp.zeros_like(done_ref)


def backward(q, k, v, u, lse, delta):
    heads, _, count = q.shape
    tokens = k.shape[2]
    per_head = lambda n: pl.BlockSpec((1, HD, n), lambda h: (h, 0, 0))
    whole = pl.BlockSpec((heads, count), lambda h: (0, 0))
    return pl.pallas_call(
        functools.partial(backward_kernel, min(256, count // 2)),
        grid=(heads,),
        in_specs=[
            per_head(count), per_head(tokens), per_head(tokens), per_head(count), whole, whole,
        ],
        out_specs=[
            pl.BlockSpec((2, 1, HD, count // 2), lambda h: (0, h, 0, 0)),
            per_head(tokens),
            per_head(tokens),
            pl.BlockSpec((8, 128), lambda h: (0, 0)),
        ],
        out_shape=[
            jax.ShapeDtypeStruct((2, heads, HD, count // 2), F32),
            jax.ShapeDtypeStruct((heads, HD, tokens), BF16),
            jax.ShapeDtypeStruct((heads, HD, tokens), BF16),
            jax.ShapeDtypeStruct((8, 128), F32),
        ],
        compiler_params=params(),
        cost_estimate=cost(40 * heads * count * tokens * HD, 9e6),
        name="attend_back",
    )(q, k, v, u, lse, delta)


def sum_kernel(pieces_ref, after_ref, out_ref):
    out_ref[...] = jnp.sum(pieces_ref[...], 0)


def sum_pieces(pieces, after):
    return pl.pallas_call(
        sum_kernel,
        out_shape=jax.ShapeDtypeStruct(pieces.shape[1:], F32),
        compiler_params=params(),
        cost_estimate=cost(pieces.size, 4 * pieces.size),
        name="sum_pieces",
    )(pieces, after)


def out_kernel(att_ref, rows_ref, own_ref, other_ref, grad_ref, keep_ref, send_ref):
    att = att_ref[0].reshape(own_ref.shape[1], att_ref.shape[3]).astype(BF16)
    term = dot(rows_ref[...], att, NT)

    @pl.when(pl.program_id(0) == 0)
    def _():
        grad_ref[...] = term

    @pl.when(pl.program_id(0) > 0)
    def _():
        grad_ref[...] += term

    send_ref[...] = dot(other_ref[...], att)
    keep_ref[...] = dot(own_ref[...], att)


def out_step(att, rows, own, other):
    _, heads, _, half = att.shape
    width, inner = own.shape
    share = rows.shape[0]
    whole = lambda a: pl.BlockSpec(a.shape, lambda i: (0, 0))
    return pl.pallas_call(
        out_kernel,
        grid=(2,),
        in_specs=[
            pl.BlockSpec((1, heads, HD, half), lambda i: (i, 0, 0, 0)),
            pl.BlockSpec((share, half), lambda i: (0, i)),
            whole(own),
            whole(other),
        ],
        out_specs=[
            pl.BlockSpec((share, inner), lambda i: (0, 0)),
            pl.BlockSpec((width, half), lambda i: (0, i)),
            pl.BlockSpec((width, half), lambda i: (0, i)),
        ],
        out_shape=[
            jax.ShapeDtypeStruct((share, inner), F32),
            jax.ShapeDtypeStruct((width, 2 * half), F32),
            jax.ShapeDtypeStruct((width, 2 * half), F32),
        ],
        compiler_params=params(),
        cost_estimate=cost(8 * half * inner * width, 12e6),
        name="project_out",
    )(att, rows, own, other)


def query_kernel(pieces_ref, norm_ref, total_ref, grad_ref):
    total = jnp.sum(pieces_ref[...], 0)
    total_ref[...] = total
    proj = (total * HD ** (-0.5)).astype(BF16)
    grad_ref[...] = dot(norm_ref[...], proj, NT)


def query_step(pieces, norm):
    _, depth, half = pieces.shape
    width = norm.shape[0]
    return pl.pallas_call(
        query_kernel,
        out_shape=[
            jax.ShapeDtypeStruct((depth, half), F32),
            jax.ShapeDtypeStruct((width, depth), F32),
        ],
        compiler_params=params(),
        cost_estimate=cost(2 * half * width * depth, 6e6),
        name="query_grad",
    )(pieces, norm)


def latent_kernel(pieces_ref, qw_ref, latents_ref, cot_ref, out_ref):
    heads, depth, rows = pieces_ref.shape
    proj = pieces_ref[...].reshape(heads * depth, rows) * HD ** (-0.5)
    up = dot(proj.T.astype(BF16), qw_ref[...])
    hat, inv = layer_norm(latents_ref[...].astype(F32))
    term = norm_backward(hat, inv, up) + cot_ref[...].astype(F32) / 2
    size = out_ref.shape[2]
    for block in range(out_ref.shape[0]):
        out_ref[block] = term[:, block * size : (block + 1) * size]


def latent_step(pieces, qw, latents, cot, blocks):
    rows, width = latents.shape
    return pl.pallas_call(
        latent_kernel,
        out_shape=jax.ShapeDtypeStruct((blocks, rows, width // blocks), F32),
        compiler_params=params(),
        cost_estimate=cost(2 * rows * qw.size, 4e6),
        name="latent_grad",
    )(pieces, qw, latents, cot)


def shift(value, axis, by, side=None, minor=True):
    size = lax.axis_size(axis)
    if side is None:
        pairs = [(i, (i + by) % size) for i in range(size)]
    elif minor:
        pairs = [(i, i // side * side + (i % side + by) % side) for i in range(size)]
    else:
        pairs = [(i, (i + by * side) % size) for i in range(size)]
    return lax.ppermute(value, axis, pairs)


def pick(blocks, index):
    return lax.dynamic_index_in_dim(blocks, index, 0, False)


def scatter_sum(blocks, axis, place):
    size = blocks.shape[0]
    total = pick(blocks, place)
    for by in range(1, size):
        total = total + shift(pick(blocks, (place + by) % size), axis, by)
    return total


def relay_sum(blocks, place, cut, send):
    far = pick(blocks, (place + 2) % 4)
    front = send(far[:cut], 1)
    back = send(far[cut:], -1)
    ahead = pick(blocks, (place + 1) % 4)
    behind = pick(blocks, (place + 3) % 4)
    ahead = jnp.concatenate([ahead[:cut] + front, ahead[cut:]], 0)
    behind = jnp.concatenate([behind[:cut], behind[cut:] + back], 0)
    return pick(blocks, place) + send(ahead, 1) + send(behind, -1)


def merge_stats(stats, side, minor):
    parts = [stats] + [shift(stats, "seq", by, side, minor) for by in range(1, side)]
    top = functools.reduce(jnp.maximum, [p[0] for p in parts])
    factors = [jnp.exp(p[0] - top) for p in parts]
    total = sum(p[1] * f for p, f in zip(parts, factors))
    delta = sum(p[2] * f for p, f in zip(parts, factors))
    return jnp.stack([top, total, delta])


def local(media_tokens, latents, query_weight, key_weight, value_weight, out_weight, cotangent):
    inner = query_weight.shape[1]
    width = query_weight.shape[0]
    heads = inner // HD
    count = latents.shape[0]
    half = count // 2
    seq, tp, dp = (lax.axis_index(a) for a in ("seq", "tp", "dp"))
    seqs, tps, dps = (lax.axis_size(a) for a in ("seq", "tp", "dp"))
    side = 4
    share = width // seqs
    part = share // dps
    padded = -(-part // 8) * 8
    rows = count // seqs
    upstream = cotangent[0]
    query_turned = query_weight.T

    media_norm, latent_norm, q, k, v, u = project(
        media_tokens[0], latents, upstream, query_turned, key_weight.T, value_weight.T, out_weight
    )
    weighted, stats = forward(q, k, v, u)

    near = merge_stats(stats, side, True)
    near, media_norm, latent_norm, cot, base, mix = lax.optimization_barrier(
        (near, media_norm, latent_norm, upstream, latents, out_weight)
    )
    blocks = media_norm.reshape(seqs, dps, part, -1).transpose(1, 0, 2, 3)
    blocks = jnp.pad(blocks, ((0, 0), (0, 0), (0, padded - part), (0, 0)))
    ready = (
        blocks.reshape(dps * seqs * padded, -1),
        lax.dynamic_slice_in_dim(latent_norm, seq // heads * half, half, 1),
        lax.dynamic_slice_in_dim(cot, seq * share, share, 1).T,
        lax.dynamic_slice_in_dim(mix, tp * inner, inner, 1).T,
        lax.dynamic_slice_in_dim(mix, (1 - tp) * inner, inner, 1).T,
        lax.dynamic_slice_in_dim(base, tp * inner, inner, 1).T,
        lax.dynamic_slice_in_dim(base, seq * rows, rows, 0),
        lax.dynamic_slice_in_dim(cot, seq * rows, rows, 0),
    )
    whole, ready = lax.optimization_barrier((merge_stats(near, side, False), ready))
    media_rows, norm_half, cot_cols, own, other, latent_cols, latent_rows, cot_rows = ready
    top, total, delta = whole
    lse = top + jnp.log(total)
    delta = delta / total
    factor = (jnp.exp(stats[0] - top) / total).reshape(heads, 2, 1, half).transpose(1, 0, 2, 3)

    scaled = (weighted * factor).reshape(seqs, HD, half)
    attended_pieces = lax.all_to_all(scaled, "seq", 0, 0, tiled=True)
    dq, dk, dv, done = backward(q, k, v, u, lse, delta)

    query_pieces = lax.all_to_all(dq.reshape(seqs, HD, half), "seq", 0, 0, tiled=True)

    ring = lambda value, by: shift(value, "dp", by)

    def weight_grad(grads):
        term = dot(media_rows, grads.reshape(inner, -1), NT)
        term = relay_sum(term.reshape(dps, seqs * padded, inner), dp, seqs * padded // 2, ring)
        return term.reshape(seqs, padded, inner)

    key_rows, value_rows = weight_grad(dk), weight_grad(dv)
    grad_key = jnp.sum(lax.all_to_all(key_rows, "seq", 0, 0, tiled=True), 0)[:part]
    grad_value = jnp.sum(lax.all_to_all(value_rows, "seq", 0, 0, tiled=True), 0)[:part]

    attended = lax.all_gather(sum_pieces(attended_pieces, done), "seq")
    out_rows, keep, away = out_step(attended.reshape(2, heads, HD, half), cot_cols, own, other)
    arrived = lax.ppermute(away, "tp", [(0, 1), (1, 0)])
    resampled = (latent_cols.astype(F32) + (keep + arrived)).astype(BF16).T[None]
    grad_out = scatter_sum(out_rows.reshape(dps, part, inner), "dp", dp).T

    query_total, term = query_step(query_pieces, norm_half)
    strips = query_total.reshape(HD, heads, rows).transpose(1, 0, 2)
    groups = [list(range(i * heads, (i + 1) * heads)) for i in range(2)]
    strips = lax.all_to_all(strips, "seq", 0, 0, axis_index_groups=groups, tiled=True)
    blocks = lax.all_to_all(term.reshape(seqs, share, HD), "seq", 0, 0, tiled=True)
    blocks = jnp.sum(blocks.reshape(2, heads, share, HD), 0).transpose(1, 0, 2)
    grad_query = scatter_sum(blocks.reshape(dps, part, inner), "dp", dp)
    term = latent_step(strips, query_turned, latent_rows, cot_rows, tps * dps)
    grad_latents = jnp.sum(lax.all_to_all(term, ("tp", "dp"), 0, 0, tiled=True), 0)
    return (resampled, grad_latents, grad_query, grad_key, grad_value, grad_out)


def solution(mesh):
    placed = (
        P("dp", "seq", None),
        P(),
        P(None, "tp"),
        P(None, "tp"),
        P(None, "tp"),
        P("tp", None),
        P("dp", None, None),
    )
    return jax.shard_map(
        local,
        mesh=mesh,
        in_specs=placed,
        out_specs=(
            P("dp", None, "tp"),
            P("seq", ("tp", "dp")),
            P(("seq", "dp"), "tp"),
            P(("seq", "dp"), "tp"),
            P(("seq", "dp"), "tp"),
            P("tp", ("seq", "dp")),
        ),
        check_vma=False,
    )
```

time: 1210 us -> 339 us (0.28)
  blocking collectives: 301 us -> 34.1 us
  waiting for transfers between devices: 285 us -> 95 us
  local copies, waits for them, and re-layouts: 213 us -> 44.6 us
  matrix products: 143 us -> 4.85 us
  other arithmetic: 162 us -> 30.3 us
  Pallas kernels: 0 us -> 63.3 us
  starting transfers between devices: 83.1 us -> 50.9 us
    unnamed x1 -> x0, blocking collectives: 250 us -> none
    all_gather x1, waiting for transfers between devices: 211 us -> 0.01 us  [local(): attended = lax.all_gather(sum_pieces(attended_pieces, done), 'seq')]
    dot_general x66 -> x2, matrix products: 143 us -> 4.85 us  [dot(): return lax.dot_general(a, b, dims, preferred_element_type=F32)]
    dynamic_slice x51 -> x2, local copies, waits for them, and re-layouts: 133 us -> 3.18 us  [the longest x1 1.93 us: local(): lax.dynamic_slice_in_dim(cot, seq * rows, rows, 0)]
    add x39 -> x9, other arithmetic: 134 us -> 12.8 us  [the longest x2 5.08 us: relay_sum(): return pick(blocks, place) + send(ahead, 1) + send(behind, -1)]
    unnamed x25 -> x0, starting transfers between devices: 82.8 us -> none
    ppermute x0 -> x21, waiting for transfers between devices: none -> 77.3 us  [the longest x20 77.3 us: shift(): return lax.ppermute(value, axis, pairs)]
    unnamed x29 -> x1, waiting for transfers between devices: 74.6 us -> 0.02 us
  transfers between devices with their start and end apart: 28 -> 27, of which waited for: 2 -> 16; matrix products, arithmetic and copies ran while one was open for 27% -> 19% of each run, Pallas kernels for 0% -> 9%
where the time goes in v1:
time: 339 us; the launch traced here: 337 us
  waiting for transfers between devices  95 us (28%)
  Pallas kernels  63.3 us (19%)
  starting transfers between devices  50.9 us (15%)
  local copies, waits for them, and re-layouts  44.6 us (13%)
  blocking collectives  34.1 us (10%)
  other arithmetic  30.3 us (9%)
  between operations  14.4 us (4%)
  matrix products  4.85 us (1%)
    ppermute x20, waiting for transfers between devices, shift(): return lax.ppermute(value, axis, pairs)  77.3 us
    ppermute x20, starting transfers between devices, shift(): return lax.ppermute(value, axis, pairs)  27.4 us
    all_to_all x1, blocking collectives, local(): lax.all_to_all(value_rows, 'seq', 0, 0, tiled=True)  24.5 us
    pallas_call x1, Pallas kernels, forward(): pl.pallas_call(functools.partial(forward_kernel, min(256, count // 2)), g...  16.9 us
    pallas_call x1, Pallas kernels, backward(): pl.pallas_call(functools.partial(backward_kernel, min(256, count // 2)),...  15.3 us
    pallas_call x1, Pallas kernels, project(): pl.pallas_call(project_kernel, grid=(steps,), in_specs=[rows(t), rows(c),...  14.8 us
    all_to_all x1, waiting for transfers between devices, local(): lax.all_to_all(key_rows, 'seq', 0, 0, tiled=True)  10.7 us
    all_to_all x1, blocking collectives, local(): lax.all_to_all(strips, 'seq', 0, 0, axis_index_groups=groups, tiled=True)  9.69 us
  transfers between devices with their start and end apart: 27, of which 16 were waited for; matrix products, arithmetic and copies ran while one was open for 19% of the time, Pallas kernels for 9%

profile of v1, /device:TPU:0, one launch (start us, length us, event | category | flops | bytes accessed | tf_op | source)
XLA Modules:
  0.0 337.4 jit_solution(14444993037170054433)
XLA Ops:
  7.2 14.8 %project.1 = (bf16[1408,512]{1,0:T(8,128)(2,1)}, bf16[1408,1024]{1,0:T(8,128)(2,1)}, bf16[8,88,1024]{2,1,0:T(8,128)(2,1)}, bf16[8,88,512]{2,1,0:T(8,128)(2,1)}, ...) custom-call(bf16[512,1408]{1,0:T(8,128)(2,1)} %bitcast.143, bf16[1024,1408]{1,0:T(8,128)(2,1)} %latents_ref.1, ...), custom_call_target="tpu_custom_call" | custom-call | flops 6090129408 | bytes 24000000 | tf_op jit(solution)/shard_map/project/pallas_call | solution.py:74
  22.0 16.9 %attend.1 = (f32[2,8,88,512]{3,2,1,0:T(8,128)}, f32[3,8,1024]{2,1,0:T(8,128)}) custom-call(bf16[8,88,1024]{2,1,0:T(8,128)(2,1)} %get-tuple-element.38.q_ref, bf16[8,88,512]{2,1,0:T(8,128)(2,1)} %get-tuple-element.39.k_ref, bf16[8,88,512]{2,1,0:T(8,128)(2,1)} %get-tuple-element.40.v_ref, bf16[8,88,1024]{2,1,0:T(8,128)(2,1)} %get-tuple-element.41.u_ref), custom_call_target="tpu_custom_call" | custom-call | flops 5905580032 | bytes 9000000 | tf_op jit(solution)/shard_map/attend/pallas_call | solution.py:118
  51.5 4.1 %collective-permute-start.5 = (f32[3,8,1024]{2,1,0:T(8,128)S(1)}, f32[3,8,1024]{2,1,0:T(8,128)S(1)}, u32[]{:S(2)}, u32[]{:S(2)}) collective-permute-start(f32[3,8,1024]{2,1,0:T(8,128)S(1)} %pad_maximum_fusion.4), channel_id=1, source_target_pairs={{0,96},{8,104},{16,112},{24,120},{32,0},{40,8},{48,16},{56,24},{64... | collective-permute-start | bytes 294920 | tf_op jit(solution)/shard_map/ppermute | solution.py:303
  57.4 4.0 %copy.27 = bf16[704,1408]{0,1:T(8,128)(2,1)} copy(bf16[704,1408]{1,0:T(8,128)(2,1)} %ow_ref.1) | data formatting | bytes 3964928 | tf_op jit(solution)/shard_map/optimization_barrier | solution.py:360
  61.4 4.7 %copy.29 = bf16[1024,1408]{0,1:T(8,128)(2,1)} copy(bf16[1024,1408]{1,0:T(8,128)(2,1)} %latents_ref.1) | data formatting | bytes 5767168 | tf_op jit(solution)/shard_map/optimization_barrier | solution.py:360
  80.1 4.5 %all-to-all-start = ((f32[16,88,512]{2,1,0:T(8,128)}), f32[16,88,512]{2,1,0:T(8,128)}, u32[]{:S(2)}, u32[]{:S(2)}) async-start(f32[16,88,512]{2,1,0:T(8,128)} %bitcast.122), calls=%async_computation | async-start | bytes 5767168 | tf_op jit(solution)/shard_map/all_to_all | solution.py:383
  84.9 15.3 %attend_back.1 = (f32[2,8,88,512]{3,2,1,0:T(8,128)}, bf16[8,88,512]{2,1,0:T(8,128)(2,1)}, bf16[8,88,512]{2,1,0:T(8,128)(2,1)}, f32[8,128]{1,0:T(8,128)}) custom-call(bf16[8,88,1024]{2,1,0:T(8,128)(2,1)} %get-tuple-element.38.q_ref, bf16[8,88,512]{2,1,0:T(8,128)(2,1)} %get-tuple-element.39.k_ref, bf16[8,88,512]{2,1,0:T(8,128)(2,1)} %get-tuple-element.40.v_ref, ...), custom_call_target="tpu_custom_call" | custom-call | flops 14763950080 | bytes 9000000 | tf_op jit(solution)/shard_map/attend_back/pallas_call | solution.py:167
  112.9 9.4 %collective-permute-done.16 = f32[192,704]{1,0:T(8,128)} collective-permute-done((f32[192,704]{1,0:T(8,128)}, f32[192,704]{1,0:T(8,128)}, u32[]{:S(2)}, u32[]{:S(2)}) %collective-permute-start.16) | collective-permute-done | bytes 540704 | tf_op jit(solution)/shard_map/ppermute | solution.py:303
  139.5 20.2 %collective-permute-done.17 = f32[384,704]{0,1:T(8,128)} collective-permute-done((f32[384,704]{0,1:T(8,128)}, f32[384,704]{0,1:T(8,128)}, u32[]{:S(2)}, u32[]{:S(2)}) %collective-permute-start.17) | collective-permute-done | bytes 1081376 | tf_op jit(solution)/shard_map/ppermute | solution.py:303
  168.1 24.5 %all_to_all.35 = f32[16,24,704]{2,1,0:T(8,128)} all-to-all(f32[16,24,704]{2,1,0:T(8,128)} %bitcast.125), channel_id=1, replica_groups=mesh['seq'=16,'tp'=2,'dp'=4] {'seq'}, dimensions={0} | all-to-all | bytes 2162688 | tf_op jit(solution)/shard_map/all_to_all | solution.py:397
  192.5 4.5 %all-to-all-start.1 = ((f32[16,88,512]{2,1,0:T(8,128)}), f32[16,88,512]{2,1,0:T(8,128)}, u32[]{:S(2)}, u32[]{:S(2)}) async-start(f32[16,88,512]{2,1,0:T(8,128)} %bitcast.126), calls=%async_computation.1 | async-start | bytes 5767168 | tf_op jit(solution)/shard_map/all_to_all | solution.py:386
  206.5 10.2 %collective-permute-done.12 = f32[192,704]{1,0:T(8,128)S(1)} collective-permute-done((f32[192,704]{1,0:T(8,128)}, f32[192,704]{1,0:T(8,128)S(1)}, u32[]{:S(2)}, u32[]{:S(2)}) %collective-permute-start.12) | collective-permute-done | bytes 540704 | tf_op jit(solution)/shard_map/ppermute | solution.py:303
  216.9 4.2 %collective-permute-done.10 = f32[192,704]{1,0:T(8,128)} collective-permute-done((f32[192,704]{1,0:T(8,128)}, f32[192,704]{1,0:T(8,128)}, u32[]{:S(2)}, u32[]{:S(2)}) %collective-permute-start.10) | collective-permute-done | bytes 540704 | tf_op jit(solution)/shard_map/ppermute | solution.py:303
  228.7 6.6 %project_out.1 = (f32[88,704]{1,0:T(8,128)}, f32[704,1024]{1,0:T(8,128)}, f32[704,1024]{1,0:T(8,128)}) custom-call(f32[2,8,88,512]{3,2,1,0:T(8,128)} %bitcast.140, bf16[88,1024]{1,0:T(8,128)(2,1)} %copy.30.rows_ref, bf16[704,704]{1,0:T(8,128)(2,1)} %get-tuple-element.56.own_ref, bf16[704,704]{1,0:T(8,128)(2,1)} %get-tuple-element.57.other_ref), custom_call_target="tpu_custom_call" | custom-call | flops 2030043136 | bytes 12000000 | tf_op jit(solution)/shard_map/project_out/pallas_call | solution.py:226
  235.2 12.1 %collective-permute-done.13 = f32[384,704]{0,1:T(8,128)} collective-permute-done((f32[384,704]{0,1:T(8,128)S(1)}, f32[384,704]{0,1:T(8,128)}, u32[]{:S(2)}, u32[]{:S(2)}) %collective-permute-start.13) | collective-permute-done | bytes 1081376 | tf_op jit(solution)/shard_map/ppermute | solution.py:303
  247.3 3.5 %collective-permute-done.11 = f32[384,704]{0,1:T(8,128)} collective-permute-done((f32[384,704]{0,1:T(8,128)}, f32[384,704]{0,1:T(8,128)}, u32[]{:S(2)}, u32[]{:S(2)}) %collective-permute-start.11) | collective-permute-done | bytes 1081376 | tf_op jit(solution)/shard_map/ppermute | solution.py:303
  254.3 6.5 %all-to-all-start.5 = ((f32[16,24,704]{2,1,0:T(8,128)}), f32[16,24,704]{2,1,0:T(8,128)S(1)}, u32[]{:S(2)}, u32[]{:S(2)}) async-start(f32[16,24,704]{2,1,0:T(8,128)} %bitcast.124), calls=%async_computation.5 | async-start | bytes 2359296 | tf_op jit(solution)/shard_map/all_to_all | solution.py:396
  260.9 3.7 %query_grad.1 = (f32[88,512]{1,0:T(8,128)}, f32[1408,88]{1,0:T(8,128)}) custom-call(f32[16,88,512]{2,1,0:T(8,128)} %all-to-all-done.1.pieces_ref, bf16[1408,512]{1,0:T(8,128)(2,1)} %constant_dynamic-slice_fusion.2.norm_ref), custom_call_target="tpu_custom_call" | custom-call | flops 126877696 | bytes 6000000 | tf_op jit(solution)/shard_map/query_grad/pallas_call | solution.py:261
  265.6 10.7 %all-to-all-done.5 = f32[16,24,704]{2,1,0:T(8,128)S(1)} async-done(((f32[16,24,704]{2,1,0:T(8,128)}), f32[16,24,704]{2,1,0:T(8,128)S(1)}, u32[]{:S(2)}, u32[]{:S(2)}) %all-to-all-start.5) | async-done | bytes 1081376 | tf_op jit(solution)/shard_map/all_to_all | solution.py:396
  276.4 9.7 %all_to_all.36 = f32[8,88,64]{1,2,0:T(8,128)S(1)} all-to-all(f32[8,88,64]{1,2,0:T(8,128)S(1)} %bitcast.130), channel_id=1, replica_groups={{0,8,16,24,32,40,48,56},{64,72,80,88,96,104,112,120},{1,9,17,25,33,41,4..., dimensions={0} | all-to-all | bytes 360448 | tf_op jit(solution)/shard_map/all_to_all | solution.py:408
  286.1 4.3 %all-to-all-start.4 = ((f32[16,88,88]{2,1,0:T(8,128)}), f32[16,88,88]{2,1,0:T(8,128)}, u32[]{:S(2)}, u32[]{:S(2)}) async-start(f32[16,88,88]{2,1,0:T(8,128)} %bitcast.131), calls=%async_computation.4 | async-start | bytes 1441792 | tf_op jit(solution)/shard_map/all_to_all | solution.py:409
  294.6 7.0 %all-to-all-done.4 = f32[16,88,88]{2,1,0:T(8,128)} async-done(((f32[16,88,88]{2,1,0:T(8,128)}), f32[16,88,88]{2,1,0:T(8,128)}, u32[]{:S(2)}, u32[]{:S(2)}) %all-to-all-start.4) | async-done | bytes 495648 | tf_op jit(solution)/shard_map/all_to_all | solution.py:409
  301.5 3.5 %all-to-all-start.3 = ((f32[8,64,176]{2,1,0:T(8,128)}), f32[8,64,176]{2,1,0:T(8,128)S(1)}, u32[]{:S(2)}, u32[]{:S(2)}) async-start(f32[8,64,176]{2,1,0:T(8,128)} %latent_grad.1), calls=%async_computation.3 | async-start | bytes 1048576 | tf_op jit(solution)/shard_map/all_to_all | solution.py:413
  325.9 4.6 %fusion = bf16[1,1024,704]{1,2,0:T(8,128)(2,1)} fusion(f32[704,1024]{1,0:T(8,128)} %get-tuple-element.58, f32[704,1024]{1,0:T(8,128)} %collective-permute-done.6, bf16[704,1024]{1,0:T(8,128)(2,1)S(1)} %dynamic-slice_bitcast_fusion), kind=kLoop, calls=%fused_computation.1 | loop fusion | flops 2883584 | bytes 8650752 | tf_op jit(solution)/shard_map/broadcast_in_dim | solution.py:402
  (123 shorter events, 113.6 us)
Async XLA Ops:
  38.9 7.4 %collective-permute-start.2 = (f32[3,8,1024]{2,1,0:T(8,128)}, f32[3,8,1024]{2,1,0:T(8,128)S(1)}, u32[]{:S(2)}, u32[]{:S(2)}) collective-permute-start(f32[3,8,1024]{2,1,0:T(8,128)} %get-tuple-element.42), channel_id=1, source_target_pairs={{0,24},{8,0},{16,8},{24,16},{32,56},{40,32},{48,40},{56,48},{64,88... | collective-permute-start | bytes 294920 | tf_op jit(solution)/shard_map/ppermute | solution.py:303
  41.7 7.1 %collective-permute-start.1 = (f32[3,8,1024]{2,1,0:T(8,128)}, f32[3,8,1024]{2,1,0:T(8,128)S(1)}, u32[]{:S(2)}, u32[]{:S(2)}) collective-permute-start(f32[3,8,1024]{2,1,0:T(8,128)} %get-tuple-element.42), channel_id=1, source_target_pairs={{0,16},{8,24},{16,0},{24,8},{32,48},{40,56},{48,32},{56,40},{64,80... | collective-permute-start | bytes 294920 | tf_op jit(solution)/shard_map/ppermute | solution.py:303
  42.5 7.3 %collective-permute-start = (f32[3,8,1024]{2,1,0:T(8,128)}, f32[3,8,1024]{2,1,0:T(8,128)S(1)}, u32[]{:S(2)}, u32[]{:S(2)}) collective-permute-start(f32[3,8,1024]{2,1,0:T(8,128)} %get-tuple-element.42), channel_id=1, source_target_pairs={{0,8},{8,16},{16,24},{24,0},{32,40},{40,48},{48,56},{56,32},{64,72... | collective-permute-start | bytes 294920 | tf_op jit(solution)/shard_map/ppermute | solution.py:303
  51.5 23.5 %collective-permute-start.5 = (f32[3,8,1024]{2,1,0:T(8,128)S(1)}, f32[3,8,1024]{2,1,0:T(8,128)S(1)}, u32[]{:S(2)}, u32[]{:S(2)}) collective-permute-start(f32[3,8,1024]{2,1,0:T(8,128)S(1)} %pad_maximum_fusion.4), channel_id=1, source_target_pairs={{0,96},{8,104},{16,112},{24,120},{32,0},{40,8},{48,16},{56,24},{64... | collective-permute-start | bytes 294920 | tf_op jit(solution)/shard_map/ppermute | solution.py:303
  55.6 19.4 %collective-permute-start.4 = (f32[3,8,1024]{2,1,0:T(8,128)S(1)}, f32[3,8,1024]{2,1,0:T(8,128)}, u32[]{:S(2)}, u32[]{:S(2)}) collective-permute-start(f32[3,8,1024]{2,1,0:T(8,128)S(1)} %pad_maximum_fusion.4), channel_id=1, source_target_pairs={{0,64},{8,72},{16,80},{24,88},{32,96},{40,104},{48,112},{56,120},{... | collective-permute-start | bytes 294920 | tf_op jit(solution)/shard_map/ppermute | solution.py:303
  55.6 19.4 %collective-permute-start.3 = (f32[3,8,1024]{2,1,0:T(8,128)S(1)}, f32[3,8,1024]{2,1,0:T(8,128)}, u32[]{:S(2)}, u32[]{:S(2)}) collective-permute-start(f32[3,8,1024]{2,1,0:T(8,128)S(1)} %pad_maximum_fusion.4), channel_id=1, source_target_pairs={{0,32},{8,40},{16,48},{24,56},{32,64},{40,72},{48,80},{56,88},{64,... | collective-permute-start | bytes 294920 | tf_op jit(solution)/shard_map/ppermute | solution.py:303
  80.1 50.0 %all-to-all-start = ((f32[16,88,512]{2,1,0:T(8,128)}), f32[16,88,512]{2,1,0:T(8,128)}, u32[]{:S(2)}, u32[]{:S(2)}) async-start(f32[16,88,512]{2,1,0:T(8,128)} %bitcast.122), calls=%async_computation | async-start | bytes 5767168 | tf_op jit(solution)/shard_map/all_to_all | solution.py:383
  84.6 144.0 %all-gather.3.cloned.1.call-start = ((), (), s32[]{:S(2)}) async-start(), calls=%async_computation.7 | async-start | bytes 3063808 | tf_op jit(solution)/shard_map/all_gather | solution.py:399
  107.7 14.6 %collective-permute-start.16 = (f32[192,704]{1,0:T(8,128)}, f32[192,704]{1,0:T(8,128)}, u32[]{:S(2)}, u32[]{:S(2)}) collective-permute-start(f32[192,704]{1,0:T(8,128)} %copy.41), channel_id=1, source_target_pairs={{0,3},{1,0},{2,1},{3,2},{4,7},{5,4},{6,5},{7,6},{8,11},{9,8},{10,9... | collective-permute-start | bytes 1622024 | tf_op jit(solution)/shard_map/ppermute | solution.py:303
  112.9 15.0 %collective-permute-start.14 = (f32[192,704]{1,0:T(8,128)}, f32[192,704]{1,0:T(8,128)}, u32[]{:S(2)}, u32[]{:S(2)}) collective-permute-start(f32[192,704]{1,0:T(8,128)} %copy.39), channel_id=1, source_target_pairs={{0,1},{1,2},{2,3},{3,0},{4,5},{5,6},{6,7},{7,4},{8,9},{9,10},{10,1... | collective-permute-start | bytes 1622024 | tf_op jit(solution)/shard_map/ppermute | solution.py:303
  136.2 23.4 %collective-permute-start.17 = (f32[384,704]{0,1:T(8,128)}, f32[384,704]{0,1:T(8,128)}, u32[]{:S(2)}, u32[]{:S(2)}) collective-permute-start(f32[384,704]{0,1:T(8,128)} %pad_maximum_fusion.3), channel_id=1, source_target_pairs={{0,3},{1,0},{2,1},{3,2},{4,7},{5,4},{6,5},{7,6},{8,11},{9,8},{10,9... | collective-permute-start | bytes 3244040 | tf_op jit(solution)/shard_map/ppermute | solution.py:303
  137.7 24.7 %collective-permute-start.15 = (f32[384,704]{0,1:T(8,128)}, f32[384,704]{0,1:T(8,128)}, u32[]{:S(2)}, u32[]{:S(2)}) collective-permute-start(f32[384,704]{0,1:T(8,128)} %pad_maximum_fusion.2), channel_id=1, source_target_pairs={{0,1},{1,2},{2,3},{3,0},{4,5},{5,6},{6,7},{7,4},{8,9},{9,10},{10,1... | collective-permute-start | bytes 3244040 | tf_op jit(solution)/shard_map/ppermute | solution.py:303
  192.5 61.8 %all-to-all-start.1 = ((f32[16,88,512]{2,1,0:T(8,128)}), f32[16,88,512]{2,1,0:T(8,128)}, u32[]{:S(2)}, u32[]{:S(2)}) async-start(f32[16,88,512]{2,1,0:T(8,128)} %bitcast.126), calls=%async_computation.1 | async-start | bytes 5767168 | tf_op jit(solution)/shard_map/all_to_all | solution.py:386
  203.1 13.5 %collective-permute-start.12 = (f32[192,704]{1,0:T(8,128)}, f32[192,704]{1,0:T(8,128)S(1)}, u32[]{:S(2)}, u32[]{:S(2)}) collective-permute-start(f32[192,704]{1,0:T(8,128)} %copy.36), channel_id=1, source_target_pairs={{0,3},{1,0},{2,1},{3,2},{4,7},{5,4},{6,5},{7,6},{8,11},{9,8},{10,9... | collective-permute-start | bytes 1622024 | tf_op jit(solution)/shard_map/ppermute | solution.py:303
  206.4 14.7 %collective-permute-start.10 = (f32[192,704]{1,0:T(8,128)}, f32[192,704]{1,0:T(8,128)}, u32[]{:S(2)}, u32[]{:S(2)}) collective-permute-start(f32[192,704]{1,0:T(8,128)} %copy.34), channel_id=1, source_target_pairs={{0,1},{1,2},{2,3},{3,0},{4,5},{5,6},{6,7},{7,4},{8,9},{9,10},{10,1... | collective-permute-start | bytes 1622024 | tf_op jit(solution)/shard_map/ppermute | solution.py:303
  224.4 22.9 %collective-permute-start.13 = (f32[384,704]{0,1:T(8,128)S(1)}, f32[384,704]{0,1:T(8,128)}, u32[]{:S(2)}, u32[]{:S(2)}) collective-permute-start(f32[384,704]{0,1:T(8,128)S(1)} %pad_maximum_fusion.1), channel_id=1, source_target_pairs={{0,3},{1,0},{2,1},{3,2},{4,7},{5,4},{6,5},{7,6},{8,11},{9,8},{10,9... | collective-permute-start | bytes 3244040 | tf_op jit(solution)/shard_map/ppermute | solution.py:303
  226.6 24.3 %collective-permute-start.11 = (f32[384,704]{0,1:T(8,128)}, f32[384,704]{0,1:T(8,128)}, u32[]{:S(2)}, u32[]{:S(2)}) collective-permute-start(f32[384,704]{0,1:T(8,128)} %pad_maximum_fusion), channel_id=1, source_target_pairs={{0,1},{1,2},{2,3},{3,0},{4,5},{5,6},{6,7},{7,4},{8,9},{9,10},{10,1... | collective-permute-start | bytes 3244040 | tf_op jit(solution)/shard_map/ppermute | solution.py:303
  235.2 90.7 %collective-permute-start.6 = (f32[704,1024]{1,0:T(8,128)}, f32[704,1024]{1,0:T(8,128)}, u32[]{:S(2)}, u32[]{:S(2)}) collective-permute-start(f32[704,1024]{1,0:T(8,128)} %get-tuple-element.59), channel_id=1, source_target_pairs={{0,4},{4,0},{1,5},{5,1},{2,6},{6,2},{3,7},{7,3},{8,12},{12,8},{9,1... | collective-permute-start | bytes 8650760 | tf_op jit(solution)/shard_map/ppermute | solution.py:401
  254.3 22.0 %all-to-all-start.5 = ((f32[16,24,704]{2,1,0:T(8,128)}), f32[16,24,704]{2,1,0:T(8,128)S(1)}, u32[]{:S(2)}, u32[]{:S(2)}) async-start(f32[16,24,704]{2,1,0:T(8,128)} %bitcast.124), calls=%async_computation.5 | async-start | bytes 2359296 | tf_op jit(solution)/shard_map/all_to_all | solution.py:396
  286.1 15.5 %all-to-all-start.4 = ((f32[16,88,88]{2,1,0:T(8,128)}), f32[16,88,88]{2,1,0:T(8,128)}, u32[]{:S(2)}, u32[]{:S(2)}) async-start(f32[16,88,88]{2,1,0:T(8,128)} %bitcast.131), calls=%async_computation.4 | async-start | bytes 1441792 | tf_op jit(solution)/shard_map/all_to_all | solution.py:409
  301.5 13.8 %all-to-all-start.3 = ((f32[8,64,176]{2,1,0:T(8,128)}), f32[8,64,176]{2,1,0:T(8,128)S(1)}, u32[]{:S(2)}, u32[]{:S(2)}) async-start(f32[8,64,176]{2,1,0:T(8,128)} %latent_grad.1), calls=%async_computation.3 | async-start | bytes 1048576 | tf_op jit(solution)/shard_map/all_to_all | solution.py:413
  309.9 6.8 %collective-permute-start.7 = (f32[22,704]{1,0:T(8,128)}, f32[22,704]{1,0:T(8,128)S(1)}, u32[]{:S(2)}, u32[]{:S(2)}) collective-permute-start(f32[22,704]{1,0:T(8,128)} %get-tuple-element.91), channel_id=1, source_target_pairs={{0,1},{1,2},{2,3},{3,0},{4,5},{5,6},{6,7},{7,4},{8,9},{9,10},{10,1... | collective-permute-start | bytes 185864 | tf_op jit(solution)/shard_map/ppermute | solution.py:303
  311.8 7.6 %collective-permute-start.9 = (f32[22,704]{1,0:T(8,128)S(1)}, f32[22,704]{1,0:T(8,128)S(1)}, u32[]{:S(2)}, u32[]{:S(2)}) collective-permute-start(f32[22,704]{1,0:T(8,128)S(1)} %get-tuple-element.92), channel_id=1, source_target_pairs={{0,3},{1,0},{2,1},{3,2},{4,7},{5,4},{6,5},{7,6},{8,11},{9,8},{10,9... | collective-permute-start | bytes 185864 | tf_op jit(solution)/shard_map/ppermute | solution.py:303
  313.1 6.4 %collective-permute-start.8 = (f32[22,704]{1,0:T(8,128)S(1)}, f32[22,704]{1,0:T(8,128)S(1)}, u32[]{:S(2)}, u32[]{:S(2)}) collective-permute-start(f32[22,704]{1,0:T(8,128)S(1)} %get-tuple-element.93), channel_id=1, source_target_pairs={{0,2},{1,3},{2,0},{3,1},{4,6},{5,7},{6,4},{7,5},{8,10},{9,11},{10,... | collective-permute-start | bytes 185864 | tf_op jit(solution)/shard_map/ppermute | solution.py:303
  (17 other events, 112.0 us)
Sparse Core Ops, SparseCore 0:
  132.9 52.5 all-gather.2

commit v2 on v1

--- a/solution.py
+++ b/solution.py
@@ -248,22 +248,26 @@
     )(att, rows, own, other)
 
 
-def query_kernel(pieces_ref, norm_ref, total_ref, grad_ref):
+def query_kernel(pieces_ref, norm_ref, out_ref):
+    places, share, _ = out_ref.shape
+    heads = places // 2
     total = jnp.sum(pieces_ref[...], 0)
-    total_ref[...] = total
+    depth, half = total.shape
+    rows = half // heads
     proj = (total * HD ** (-0.5)).astype(BF16)
-    grad_ref[...] = dot(norm_ref[...], proj, NT)
-
-
-def query_step(pieces, norm):
+    term = dot(norm_ref[...], proj, NT)
+    for place in range(places):
+        strip = place % heads * rows
+        out_ref[place, :, :depth] = term[place * share : (place + 1) * share, :]
+        out_ref[place, :depth, 128 : 128 + rows] = total[:, strip : strip + rows]
+
+
+def query_step(pieces, norm, places):
     _, depth, half = pieces.shape
     width = norm.shape[0]
     return pl.pallas_call(
         query_kernel,
-        out_shape=[
-            jax.ShapeDtypeStruct((depth, half), F32),
-            jax.ShapeDtypeStruct((width, depth), F32),
-        ],
+        out_shape=jax.ShapeDtypeStruct((places, width // places, 256), F32),
         compiler_params=params(),
         cost_estimate=cost(2 * half * width * depth, 6e6),
         name="query_grad",
@@ -346,7 +350,6 @@
     side = 4
     share = width // seqs
     part = share // dps
-    padded = -(-part // 8) * 8
     rows = count // seqs
     upstream = cotangent[0]
     query_turned = query_weight.T
@@ -356,25 +359,7 @@
     )
     weighted, stats = forward(q, k, v, u)
 
-    near = merge_stats(stats, side, True)
-    near, media_norm, latent_norm, cot, base, mix = lax.optimization_barrier(
-        (near, media_norm, latent_norm, upstream, latents, out_weight)
-    )
-    blocks = media_norm.reshape(seqs, dps, part, -1).transpose(1, 0, 2, 3)
-    blocks = jnp.pad(blocks, ((0, 0), (0, 0), (0, padded - part), (0, 0)))
-    ready = (
-        blocks.reshape(dps * seqs * padded, -1),
-        lax.dynamic_slice_in_dim(latent_norm, seq // heads * half, half, 1),
-        lax.dynamic_slice_in_dim(cot, seq * share, share, 1).T,
-        lax.dynamic_slice_in_dim(mix, tp * inner, inner, 1).T,
-        lax.dynamic_slice_in_dim(mix, (1 - tp) * inner, inner, 1).T,
-        lax.dynamic_slice_in_dim(base, tp * inner, inner, 1).T,
-        lax.dynamic_slice_in_dim(base, seq * rows, rows, 0),
-        lax.dynamic_slice_in_dim(cot, seq * rows, rows, 0),
-    )
-    whole, ready = lax.optimization_barrier((merge_stats(near, side, False), ready))
-    media_rows, norm_half, cot_cols, own, other, latent_cols, latent_rows, cot_rows = ready
-    top, total, delta = whole
+    top, total, delta = merge_stats(merge_stats(stats, side, True), side, False)
     lse = top + jnp.log(total)
     delta = delta / total
     factor = (jnp.exp(stats[0] - top) / total).reshape(heads, 2, 1, half).transpose(1, 0, 2, 3)
@@ -385,31 +370,39 @@
 
     query_pieces = lax.all_to_all(dq.reshape(seqs, HD, half), "seq", 0, 0, tiled=True)
 
-    ring = lambda value, by: shift(value, "dp", by)
-
-    def weight_grad(grads):
-        term = dot(media_rows, grads.reshape(inner, -1), NT)
-        term = relay_sum(term.reshape(dps, seqs * padded, inner), dp, seqs * padded // 2, ring)
-        return term.reshape(seqs, padded, inner)
-
-    key_rows, value_rows = weight_grad(dk), weight_grad(dv)
-    grad_key = jnp.sum(lax.all_to_all(key_rows, "seq", 0, 0, tiled=True), 0)[:part]
-    grad_value = jnp.sum(lax.all_to_all(value_rows, "seq", 0, 0, tiled=True), 0)[:part]
+    major, minor = seq // side, seq % side
+    cut = share // 16 * 8
+    along = lambda value, by: shift(value, "seq", by, side, True)
+    across = lambda value, by: shift(value, "seq", by, side, False)
+    key_term = dot(media_norm, dk.reshape(inner, -1), NT).reshape(side, side, share, inner)
+    value_term = dot(media_norm, dv.reshape(inner, -1), NT).reshape(side, side, share, inner)
+    key_rows = relay_sum(key_term.transpose(1, 0, 2, 3), minor, side // 2, along)
+    value_rows = relay_sum(value_term, major, side // 2, across)
+    key_rows = relay_sum(key_rows, major, cut, across)
+    value_rows = relay_sum(value_rows, minor, cut, along)
+    both = jnp.stack([key_rows, value_rows]).reshape(2, dps, part, inner).transpose(1, 0, 2, 3)
+    grad_key, grad_value = scatter_sum(both, "dp", dp)
 
     attended = lax.all_gather(sum_pieces(attended_pieces, done), "seq")
+    cot_cols = lax.dynamic_slice_in_dim(upstream, seq * share, share, 1).T
+    own = lax.dynamic_slice_in_dim(out_weight, tp * inner, inner, 1).T
+    other = lax.dynamic_slice_in_dim(out_weight, (1 - tp) * inner, inner, 1).T
+    latent_cols = lax.dynamic_slice_in_dim(latents, tp * inner, inner, 1).T
     out_rows, keep, away = out_step(attended.reshape(2, heads, HD, half), cot_cols, own, other)
     arrived = lax.ppermute(away, "tp", [(0, 1), (1, 0)])
     resampled = (latent_cols.astype(F32) + (keep + arrived)).astype(BF16).T[None]
     grad_out = scatter_sum(out_rows.reshape(dps, part, inner), "dp", dp).T
 
-    query_total, term = query_step(query_pieces, norm_half)
-    strips = query_total.reshape(HD, heads, rows).transpose(1, 0, 2)
-    groups = [list(range(i * heads, (i + 1) * heads)) for i in range(2)]
-    strips = lax.all_to_all(strips, "seq", 0, 0, axis_index_groups=groups, tiled=True)
-    blocks = lax.all_to_all(term.reshape(seqs, share, HD), "seq", 0, 0, tiled=True)
-    blocks = jnp.sum(blocks.reshape(2, heads, share, HD), 0).transpose(1, 0, 2)
+    side_of = seq // heads
+    norm_half = lax.dynamic_slice_in_dim(latent_norm, side_of * half, half, 1)
+    sent = query_step(query_pieces, norm_half, seqs)
+    sent = lax.all_to_all(sent, "seq", 0, 0, tiled=True)
+    strips = lax.dynamic_slice(sent, (side_of * heads, 0, 128), (heads, HD, rows))
+    latent_rows = lax.dynamic_slice_in_dim(latents, seq * rows, rows, 0)
+    cot_rows = lax.dynamic_slice_in_dim(upstream, seq * rows, rows, 0)
+    term = latent_step(strips, query_turned, latent_rows, cot_rows, tps * dps)
+    blocks = (sent[:heads, :, :HD] + sent[heads:, :, :HD]).transpose(1, 0, 2)
     grad_query = scatter_sum(blocks.reshape(dps, part, inner), "dp", dp)
-    term = latent_step(strips, query_turned, latent_rows, cot_rows, tps * dps)
     grad_latents = jnp.sum(lax.all_to_all(term, ("tp", "dp"), 0, 0, tiled=True), 0)
     return (resampled, grad_latents, grad_query, grad_key, grad_value, grad_out)
 

time: 339 us -> 300 us (0.88)
  blocking collectives: 34.1 us -> 0 us
  starting transfers between devices: 50.9 us -> 66.6 us
  local copies, waits for them, and re-layouts: 44.6 us -> 32 us
  waiting for transfers between devices: 95 us -> 86.4 us
    all_to_all x2 -> x0, blocking collectives: 34.1 us -> none  [the longest x1 24.5 us: local(): lax.all_to_all(value_rows, 'seq', 0, 0, tiled=True)]
    ppermute x20 -> x31, starting transfers between devices: 27.4 us -> 48.1 us  [shift(): return lax.ppermute(value, axis, pairs)]
    dynamic_slice x2 -> x9, local copies, waits for them, and re-layouts: 3.18 us -> 13.6 us  [the longest x1 4.09 us: local(): other = lax.dynamic_slice_in_dim(out_weight, (1 - tp) * inner, inner, 1).T]
    unnamed x29 -> x32, local copies, waits for them, and re-layouts: 4.64 us -> 15 us
    optimization_barrier x3 -> x0, local copies, waits for them, and re-layouts: 9.51 us -> none  [the longest x2 8.69 us: local(): lax.optimization_barrier((near, media_norm, latent_norm, upstream, latent...]
    all_to_all x2 -> x1, waiting for transfers between devices: 17.7 us -> 8.79 us  [local(): sent = lax.all_to_all(sent, 'seq', 0, 0, tiled=True)]
    all_to_all x1, waiting for transfers between devices: 0.01 us -> 7.49 us  [local(): attended_pieces = lax.all_to_all(scaled, 'seq', 0, 0, tiled=True)]
    ppermute x20 -> x31, waiting for transfers between devices: 77.3 us -> 70.1 us  [shift(): return lax.ppermute(value, axis, pairs)]
  transfers between devices with their start and end apart: 27 -> 37, of which waited for: 16 -> 21; matrix products, arithmetic and copies ran while one was open for 19% -> 17% of each run, Pallas kernels for 9% -> 11%
where the time goes in v2:
time: 300 us; the launch traced here: 299 us
  waiting for transfers between devices  86.4 us (29%)
  starting transfers between devices  66.6 us (22%)
  Pallas kernels  63.4 us (21%)
  local copies, waits for them, and re-layouts  32 us (11%)
  other arithmetic  30.5 us (10%)
  between operations  14.5 us (5%)
  matrix products  5.32 us (2%)
    ppermute x31, waiting for transfers between devices, shift(): return lax.ppermute(value, axis, pairs)  70.1 us
    ppermute x31, starting transfers between devices, shift(): return lax.ppermute(value, axis, pairs)  48.1 us
    pallas_call x1, Pallas kernels, forward(): pl.pallas_call(functools.partial(forward_kernel, min(256, count // 2)), g...  16.8 us
    pallas_call x1, Pallas kernels, backward(): pl.pallas_call(functools.partial(backward_kernel, min(256, count // 2)),...  15.4 us
    unnamed x32, local copies, waits for them, and re-layouts  15 us
    pallas_call x1, Pallas kernels, project(): pl.pallas_call(project_kernel, grid=(steps,), in_specs=[rows(t), rows(c),...  14.9 us
    all_to_all x1, waiting for transfers between devices, local(): sent = lax.all_to_all(sent, 'seq', 0, 0, tiled=True)  8.79 us
    all_to_all x1, waiting for transfers between devices, local(): attended_pieces = lax.all_to_all(scaled, 'seq', 0, 0, tiled=True)  7.49 us
  transfers between devices with their start and end apart: 37, of which 21 were waited for; matrix products, arithmetic and copies ran while one was open for 17% of the time, Pallas kernels for 11%

profile of v2, /device:TPU:0, one launch (start us, length us, event | category | flops | bytes accessed | tf_op | source)
XLA Modules:
  0.0 298.7 jit_solution(1847258681152497836)
XLA Ops:
  7.2 14.9 %project.1 = (bf16[1408,512]{1,0:T(8,128)(2,1)}, bf16[1408,1024]{1,0:T(8,128)(2,1)}, bf16[8,88,1024]{2,1,0:T(8,128)(2,1)}, bf16[8,88,512]{2,1,0:T(8,128)(2,1)}, ...) custom-call(bf16[512,1408]{1,0:T(8,128)(2,1)} %bitcast.496, bf16[1024,1408]{1,0:T(8,128)(2,1)} %latents_ref.1, ...), custom_call_target="tpu_custom_call" | custom-call | flops 6090129408 | bytes 24000000 | tf_op jit(solution)/shard_map/project/pallas_call | solution.py:74
  22.0 16.8 %attend.1 = (f32[2,8,88,512]{3,2,1,0:T(8,128)}, f32[3,8,1024]{2,1,0:T(8,128)}) custom-call(bf16[8,88,1024]{2,1,0:T(8,128)(2,1)} %get-tuple-element.21.q_ref, bf16[8,88,512]{2,1,0:T(8,128)(2,1)} %get-tuple-element.22.k_ref, bf16[8,88,512]{2,1,0:T(8,128)(2,1)} %get-tuple-element.23.v_ref, bf16[8,88,1024]{2,1,0:T(8,128)(2,1)} %get-tuple-element.24.u_ref), custom_call_target="tpu_custom_call" | custom-call | flops 5905580032 | bytes 9000000 | tf_op jit(solution)/shard_map/attend/pallas_call | solution.py:118
  51.4 4.1 %collective-permute-start.5 = (f32[3,8,1024]{2,1,0:T(8,128)S(1)}, f32[3,8,1024]{2,1,0:T(8,128)S(1)}, u32[]{:S(2)}, u32[]{:S(2)}) collective-permute-start(f32[3,8,1024]{2,1,0:T(8,128)S(1)} %pad_maximum_fusion.8), channel_id=1, source_target_pairs={{0,96},{8,104},{16,112},{24,120},{32,0},{40,8},{48,16},{56,24},{64... | collective-permute-start | bytes 294920 | tf_op jit(solution)/shard_map/ppermute | solution.py:307
  63.4 3.8 %broadcast_multiply_fusion = f32[2,8,88,512]{3,2,1,0:T(8,128)} fusion(f32[2,8,88,512]{3,2,1,0:T(8,128)} %get-tuple-element.25, f32[2,8,512]{2,1,0:T(8,128)S(1)} %divide_bitcast_fusion), kind=kLoop, calls=%fused_computation.3 | loop fusion | flops 720896 | bytes 5799936 | tf_op jit(solution)/shard_map/mul | solution.py:367
  67.2 3.7 %all-to-all-start = ((f32[16,88,512]{2,1,0:T(8,128)}), f32[16,88,512]{2,1,0:T(8,128)S(1)}, u32[]{:S(2)}, u32[]{:S(2)}) async-start(f32[16,88,512]{2,1,0:T(8,128)} %bitcast.467), calls=%async_computation | async-start | bytes 5767168 | tf_op jit(solution)/shard_map/all_to_all | solution.py:368
  71.2 4.1 %constant_dynamic-slice_fusion.3 = (bf16[704,704]{1,0:T(8,128)(2,1)}, bf16[704,704]{1,0:T(8,128)(2,1)}) fusion(bf16[704,1408]{1,0:T(8,128)(2,1)} %ow_ref.1, s32[]{:T(128)S(6)} %select_n.152, s32[]{:T(128)S(6)} %select_n.150), kind=kLoop, calls=%fused_computation.145 | loop fusion | bytes 3964936 | tf_op jit(solution)/shard_map/dynamic_slice | solution.py:389
  79.8 15.4 %attend_back.1 = (f32[2,8,88,512]{3,2,1,0:T(8,128)}, bf16[8,88,512]{2,1,0:T(8,128)(2,1)}, bf16[8,88,512]{2,1,0:T(8,128)(2,1)}, f32[8,128]{1,0:T(8,128)}) custom-call(bf16[8,88,1024]{2,1,0:T(8,128)(2,1)} %get-tuple-element.21.q_ref, bf16[8,88,512]{2,1,0:T(8,128)(2,1)} %get-tuple-element.22.k_ref, bf16[8,88,512]{2,1,0:T(8,128)(2,1)} %get-tuple-element.23.v_ref, ...), custom_call_target="tpu_custom_call" | custom-call | flops 14763950080 | bytes 9000000 | tf_op jit(solution)/shard_map/attend_back/pallas_call | solution.py:167
  103.4 7.5 %all-to-all-done.pieces_ref = f32[16,88,512]{2,1,0:T(8,128)S(1)} async-done(((f32[16,88,512]{2,1,0:T(8,128)}), f32[16,88,512]{2,1,0:T(8,128)S(1)}, u32[]{:S(2)}, u32[]{:S(2)}) %all-to-all-start) | async-done | bytes 2883616 | tf_op jit(solution)/shard_map/all_to_all | solution.py:368
  129.4 5.1 %collective-permute-done.12 = f32[2,88,704]{2,1,0:T(8,128)S(1)} collective-permute-done((f32[2,88,704]{2,1,0:T(8,128)S(1)}, f32[2,88,704]{2,1,0:T(8,128)S(1)}, u32[]{:S(2)}, u32[]{:S(2)}) %collective-permute-start.12) | collective-permute-done | bytes 495648 | tf_op jit(solution)/shard_map/ppermute | solution.py:307
  135.7 3.7 %collective-permute-start.13 = (f32[4,88,704]{2,1,0:T(8,128)}, f32[4,88,704]{2,1,0:T(8,128)}, u32[]{:S(2)}, u32[]{:S(2)}) collective-permute-start(f32[4,88,704]{2,1,0:T(8,128)} %pad_maximum_fusion.1), channel_id=1, source_target_pairs={{0,24},{8,0},{16,8},{24,16},{32,56},{40,32},{48,40},{56,48},{64,88... | collective-permute-start | bytes 2973704 | tf_op jit(solution)/shard_map/ppermute | solution.py:307
  144.9 5.7 %all-to-all-start.1 = ((f32[16,88,512]{2,1,0:T(8,128)}), f32[16,88,512]{2,1,0:T(8,128)S(1)}, u32[]{:S(2)}, u32[]{:S(2)}) async-start(f32[16,88,512]{2,1,0:T(8,128)} %bitcast.470), calls=%async_computation.1 | async-start | bytes 5767168 | tf_op jit(solution)/shard_map/all_to_all | solution.py:371
  159.9 4.1 %collective-permute-done.21 = f32[4,88,704]{2,1,0:T(8,128)} collective-permute-done((f32[4,88,704]{2,1,0:T(8,128)}, f32[4,88,704]{2,1,0:T(8,128)}, u32[]{:S(2)}, u32[]{:S(2)}) %collective-permute-start.21) | collective-permute-done | bytes 991264 | tf_op jit(solution)/shard_map/ppermute | solution.py:307
  164.0 6.8 %collective-permute-done.19 = f32[4,88,704]{2,1,0:T(8,128)} collective-permute-done((f32[4,88,704]{2,1,0:T(8,128)}, f32[4,88,704]{2,1,0:T(8,128)}, u32[]{:S(2)}, u32[]{:S(2)}) %collective-permute-start.19) | collective-permute-done | bytes 991264 | tf_op jit(solution)/shard_map/ppermute | solution.py:307
  173.0 3.3 %collective-permute-start.24 = (f32[48,704]{1,0:T(8,128)S(1)}, f32[48,704]{1,0:T(8,128)S(1)}, u32[]{:S(2)}, u32[]{:S(2)}) collective-permute-start(f32[48,704]{1,0:T(8,128)S(1)} %get-tuple-element.50), channel_id=1, source_target_pairs={{0,24},{8,0},{16,8},{24,16},{32,56},{40,32},{48,40},{56,48},{64,88... | collective-permute-start | bytes 405512 | tf_op jit(solution)/shard_map/ppermute | solution.py:307
  176.3 10.9 %collective-permute-done.13 = f32[4,88,704]{2,1,0:T(8,128)} collective-permute-done((f32[4,88,704]{2,1,0:T(8,128)}, f32[4,88,704]{2,1,0:T(8,128)}, u32[]{:S(2)}, u32[]{:S(2)}) %collective-permute-start.13) | collective-permute-done | bytes 991264 | tf_op jit(solution)/shard_map/ppermute | solution.py:307
  187.2 4.8 %collective-permute-done.11 = f32[4,88,704]{2,1,0:T(8,128)} collective-permute-done((f32[4,88,704]{2,1,0:T(8,128)}, f32[4,88,704]{2,1,0:T(8,128)}, u32[]{:S(2)}, u32[]{:S(2)}) %collective-permute-start.11) | collective-permute-done | bytes 991264 | tf_op jit(solution)/shard_map/ppermute | solution.py:307
  198.2 11.6 %collective-permute-done.22 = f32[40,704]{1,0:T(8,128)S(1)} collective-permute-done((f32[40,704]{1,0:T(8,128)S(1)}, f32[40,704]{1,0:T(8,128)S(1)}, u32[]{:S(2)}, u32[]{:S(2)}) %collective-permute-start.22) | collective-permute-done | bytes 112672 | tf_op jit(solution)/shard_map/ppermute | solution.py:307
  214.1 6.6 %project_out.1 = (f32[88,704]{1,0:T(8,128)}, f32[704,1024]{1,0:T(8,128)}, f32[704,1024]{1,0:T(8,128)}) custom-call(f32[2,8,88,512]{3,2,1,0:T(8,128)} %bitcast.493, bf16[88,1024]{1,0:T(8,128)(2,1)} %bitcast.477, bf16[704,704]{1,0:T(8,128)(2,1)} %bitcast.474, bf16[704,704]{1,0:T(8,128)(2,1)} %bitcast.473), custom_call_target="tpu_custom_call" | custom-call | flops 2030043136 | bytes 12000000 | tf_op jit(solution)/shard_map/project_out/pallas_call | solution.py:226
  227.2 4.0 %query_grad.1 = f32[16,88,256]{2,1,0:T(8,128)} custom-call(f32[16,88,512]{2,1,0:T(8,128)} %copy-done.2, bf16[1408,512]{1,0:T(8,128)(2,1)} %constant_dynamic-slice_fusion.2.norm_ref), custom_call_target="tpu_custom_call" | custom-call | flops 126877696 | bytes 6000000 | tf_op jit(solution)/shard_map/query_grad/pallas_call | solution.py:268
  231.2 4.2 %all-to-all-start.2 = ((f32[16,88,256]{2,1,0:T(8,128)}), f32[16,88,256]{2,1,0:T(8,128)S(1)}, u32[]{:S(2)}, u32[]{:S(2)}) async-start(f32[16,88,256]{2,1,0:T(8,128)} %query_grad.1), calls=%async_computation.2 | async-start | bytes 2883584 | tf_op jit(solution)/shard_map/all_to_all | solution.py:399
  250.0 8.8 %all-to-all-done.2 = f32[16,88,256]{2,1,0:T(8,128)S(1)} async-done(((f32[16,88,256]{2,1,0:T(8,128)}), f32[16,88,256]{2,1,0:T(8,128)S(1)}, u32[]{:S(2)}, u32[]{:S(2)}) %all-to-all-start.2) | async-done | bytes 1441824 | tf_op jit(solution)/shard_map/all_to_all | solution.py:399
  263.1 4.6 %all-to-all-start.3 = ((f32[8,64,176]{2,1,0:T(8,128)}), f32[8,64,176]{2,1,0:T(8,128)S(1)}, u32[]{:S(2)}, u32[]{:S(2)}) async-start(f32[8,64,176]{2,1,0:T(8,128)} %latent_grad.1), calls=%async_computation.3 | async-start | bytes 1048576 | tf_op jit(solution)/shard_map/all_to_all | solution.py:406
  274.0 6.1 %collective-permute-done.7 = f32[22,704]{1,0:T(8,128)S(1)} collective-permute-done((f32[22,704]{1,0:T(8,128)S(1)}, f32[22,704]{1,0:T(8,128)S(1)}, u32[]{:S(2)}, u32[]{:S(2)}) %collective-permute-start.7) | collective-permute-done | bytes 61984 | tf_op jit(solution)/shard_map/ppermute | solution.py:307
  287.2 4.6 %fusion.1 = bf16[1,1024,704]{1,2,0:T(8,128)(2,1)} fusion(f32[704,1024]{1,0:T(8,128)} %get-tuple-element.28, f32[704,1024]{1,0:T(8,128)} %collective-permute-done.6, bf16[1024,704]{0,1:T(8,128)(2,1)S(1)} %copy-done.4), kind=kLoop, calls=%fused_computation.2 | loop fusion | flops 2883584 | bytes 8650752 | tf_op jit(solution)/shard_map/broadcast_in_dim | solution.py:393
  (154 shorter events, 119.0 us)
Async XLA Ops:
  67.2 43.7 %all-to-all-start = ((f32[16,88,512]{2,1,0:T(8,128)}), f32[16,88,512]{2,1,0:T(8,128)S(1)}, u32[]{:S(2)}, u32[]{:S(2)}) async-start(f32[16,88,512]{2,1,0:T(8,128)} %bitcast.467), calls=%async_computation | async-start | bytes 5767168 | tf_op jit(solution)/shard_map/all_to_all | solution.py:368
  70.9 143.1 %all-gather.3.cloned.1.call-start = ((), (), s32[]{:S(2)}) async-start(), calls=%async_computation.4 | async-start | bytes 3063808 | tf_op jit(solution)/shard_map/all_gather | solution.py:386
  100.2 23.3 %collective-permute-start.18 = (f32[2,88,704]{2,1,0:T(8,128)}, f32[2,88,704]{2,1,0:T(8,128)}, u32[]{:S(2)}, u32[]{:S(2)}) collective-permute-start(f32[2,88,704]{2,1,0:T(8,128)} %get-tuple-element.38), channel_id=1, source_target_pairs={{0,32},{8,40},{16,48},{24,56},{32,64},{40,72},{48,80},{56,88},{64,... | collective-permute-start | bytes 1486856 | tf_op jit(solution)/shard_map/ppermute | solution.py:307
  102.0 21.5 %collective-permute-start.20 = (f32[2,88,704]{2,1,0:T(8,128)}, f32[2,88,704]{2,1,0:T(8,128)}, u32[]{:S(2)}, u32[]{:S(2)}) collective-permute-start(f32[2,88,704]{2,1,0:T(8,128)} %get-tuple-element.40), channel_id=1, source_target_pairs={{0,96},{8,104},{16,112},{24,120},{32,0},{40,8},{48,16},{56,24},{64... | collective-permute-start | bytes 1486856 | tf_op jit(solution)/shard_map/ppermute | solution.py:307
  120.1 19.4 %collective-permute-start.10 = (f32[2,88,704]{2,1,0:T(8,128)S(1)}, f32[2,88,704]{2,1,0:T(8,128)S(1)}, u32[]{:S(2)}, u32[]{:S(2)}) collective-permute-start(f32[2,88,704]{2,1,0:T(8,128)S(1)} %get-tuple-element.55), channel_id=1, source_target_pairs={{0,8},{8,16},{16,24},{24,0},{32,40},{40,48},{48,56},{56,32},{64,72... | collective-permute-start | bytes 1486856 | tf_op jit(solution)/shard_map/ppermute | solution.py:307
  120.1 14.3 %collective-permute-start.12 = (f32[2,88,704]{2,1,0:T(8,128)S(1)}, f32[2,88,704]{2,1,0:T(8,128)S(1)}, u32[]{:S(2)}, u32[]{:S(2)}) collective-permute-start(f32[2,88,704]{2,1,0:T(8,128)S(1)} %get-tuple-element.56), channel_id=1, source_target_pairs={{0,24},{8,0},{16,8},{24,16},{32,56},{40,32},{48,40},{56,48},{64,88... | collective-permute-start | bytes 1486856 | tf_op jit(solution)/shard_map/ppermute | solution.py:307
  126.3 37.7 %collective-permute-start.21 = (f32[4,88,704]{2,1,0:T(8,128)}, f32[4,88,704]{2,1,0:T(8,128)}, u32[]{:S(2)}, u32[]{:S(2)}) collective-permute-start(f32[4,88,704]{2,1,0:T(8,128)} %pad_maximum_fusion.3), channel_id=1, source_target_pairs={{0,96},{8,104},{16,112},{24,120},{32,0},{40,8},{48,16},{56,24},{64... | collective-permute-start | bytes 2973704 | tf_op jit(solution)/shard_map/ppermute | solution.py:307
  129.3 41.5 %collective-permute-start.19 = (f32[4,88,704]{2,1,0:T(8,128)}, f32[4,88,704]{2,1,0:T(8,128)}, u32[]{:S(2)}, u32[]{:S(2)}) collective-permute-start(f32[4,88,704]{2,1,0:T(8,128)} %pad_maximum_fusion.2), channel_id=1, source_target_pairs={{0,32},{8,40},{16,48},{24,56},{32,64},{40,72},{48,80},{56,88},{64,... | collective-permute-start | bytes 2973704 | tf_op jit(solution)/shard_map/ppermute | solution.py:307
  135.7 51.5 %collective-permute-start.13 = (f32[4,88,704]{2,1,0:T(8,128)}, f32[4,88,704]{2,1,0:T(8,128)}, u32[]{:S(2)}, u32[]{:S(2)}) collective-permute-start(f32[4,88,704]{2,1,0:T(8,128)} %pad_maximum_fusion.1), channel_id=1, source_target_pairs={{0,24},{8,0},{16,8},{24,16},{32,56},{40,32},{48,40},{56,48},{64,88... | collective-permute-start | bytes 2973704 | tf_op jit(solution)/shard_map/ppermute | solution.py:307
  140.6 51.5 %collective-permute-start.11 = (f32[4,88,704]{2,1,0:T(8,128)}, f32[4,88,704]{2,1,0:T(8,128)}, u32[]{:S(2)}, u32[]{:S(2)}) collective-permute-start(f32[4,88,704]{2,1,0:T(8,128)} %pad_maximum_fusion), channel_id=1, source_target_pairs={{0,8},{8,16},{16,24},{24,0},{32,40},{40,48},{48,56},{56,32},{64,72... | collective-permute-start | bytes 2973704 | tf_op jit(solution)/shard_map/ppermute | solution.py:307
  144.9 80.8 %all-to-all-start.1 = ((f32[16,88,512]{2,1,0:T(8,128)}), f32[16,88,512]{2,1,0:T(8,128)S(1)}, u32[]{:S(2)}, u32[]{:S(2)}) async-start(f32[16,88,512]{2,1,0:T(8,128)} %bitcast.470), calls=%async_computation.1 | async-start | bytes 5767168 | tf_op jit(solution)/shard_map/all_to_all | solution.py:371
  172.9 36.9 %collective-permute-start.22 = (f32[40,704]{1,0:T(8,128)S(1)}, f32[40,704]{1,0:T(8,128)S(1)}, u32[]{:S(2)}, u32[]{:S(2)}) collective-permute-start(f32[40,704]{1,0:T(8,128)S(1)} %get-tuple-element.47), channel_id=1, source_target_pairs={{0,8},{8,16},{16,24},{24,0},{32,40},{40,48},{48,56},{56,32},{64,72... | collective-permute-start | bytes 337928 | tf_op jit(solution)/shard_map/ppermute | solution.py:307
  173.0 37.9 %collective-permute-start.24 = (f32[48,704]{1,0:T(8,128)S(1)}, f32[48,704]{1,0:T(8,128)S(1)}, u32[]{:S(2)}, u32[]{:S(2)}) collective-permute-start(f32[48,704]{1,0:T(8,128)S(1)} %get-tuple-element.50), channel_id=1, source_target_pairs={{0,24},{8,0},{16,8},{24,16},{32,56},{40,32},{48,40},{56,48},{64,88... | collective-permute-start | bytes 405512 | tf_op jit(solution)/shard_map/ppermute | solution.py:307
  194.2 15.8 %collective-permute-start.14 = (f32[40,704]{1,0:T(8,128)S(1)}, f32[40,704]{1,0:T(8,128)S(1)}, u32[]{:S(2)}, u32[]{:S(2)}) collective-permute-start(f32[40,704]{1,0:T(8,128)S(1)} %get-tuple-element.51), channel_id=1, source_target_pairs={{0,32},{8,40},{16,48},{24,56},{32,64},{40,72},{48,80},{56,88},{64,... | collective-permute-start | bytes 337928 | tf_op jit(solution)/shard_map/ppermute | solution.py:307
  195.4 25.3 %collective-permute-start.16 = (f32[48,704]{1,0:T(8,128)}, f32[48,704]{1,0:T(8,128)}, u32[]{:S(2)}, u32[]{:S(2)}) collective-permute-start(f32[48,704]{1,0:T(8,128)} %get-tuple-element.54), channel_id=1, source_target_pairs={{0,96},{8,104},{16,112},{24,120},{32,0},{40,8},{48,16},{56,24},{64... | collective-permute-start | bytes 405512 | tf_op jit(solution)/shard_map/ppermute | solution.py:307
  209.9 25.5 %collective-permute-start.23 = (f32[88,704]{1,0:T(8,128)S(1)}, f32[88,704]{1,0:T(8,128)}, u32[]{:S(2)}, u32[]{:S(2)}) collective-permute-start(f32[88,704]{1,0:T(8,128)S(1)} %pad_maximum_fusion.6), channel_id=1, source_target_pairs={{0,8},{8,16},{16,24},{24,0},{32,40},{40,48},{48,56},{56,32},{64,72... | collective-permute-start | bytes 743432 | tf_op jit(solution)/shard_map/ppermute | solution.py:307
  210.1 26.5 %collective-permute-start.15 = (f32[88,704]{1,0:T(8,128)S(1)}, f32[88,704]{1,0:T(8,128)}, u32[]{:S(2)}, u32[]{:S(2)}) collective-permute-start(f32[88,704]{1,0:T(8,128)S(1)} %pad_maximum_fusion.4), channel_id=1, source_target_pairs={{0,32},{8,40},{16,48},{24,56},{32,64},{40,72},{48,80},{56,88},{64,... | collective-permute-start | bytes 743432 | tf_op jit(solution)/shard_map/ppermute | solution.py:307
  211.7 23.6 %collective-permute-start.25 = (f32[88,704]{1,0:T(8,128)}, f32[88,704]{1,0:T(8,128)}, u32[]{:S(2)}, u32[]{:S(2)}) collective-permute-start(f32[88,704]{1,0:T(8,128)} %pad_maximum_fusion.7), channel_id=1, source_target_pairs={{0,24},{8,0},{16,8},{24,16},{32,56},{40,32},{48,40},{56,48},{64,88... | collective-permute-start | bytes 743432 | tf_op jit(solution)/shard_map/ppermute | solution.py:307
  220.7 66.5 %collective-permute-start.6 = (f32[704,1024]{1,0:T(8,128)}, f32[704,1024]{1,0:T(8,128)}, u32[]{:S(2)}, u32[]{:S(2)}) collective-permute-start(f32[704,1024]{1,0:T(8,128)} %get-tuple-element.29), channel_id=1, source_target_pairs={{0,4},{4,0},{1,5},{5,1},{2,6},{6,2},{3,7},{7,3},{8,12},{12,8},{9,1... | collective-permute-start | bytes 8650760 | tf_op jit(solution)/shard_map/ppermute | solution.py:392
  222.4 14.1 %collective-permute-start.17 = (f32[88,704]{1,0:T(8,128)}, f32[88,704]{1,0:T(8,128)}, u32[]{:S(2)}, u32[]{:S(2)}) collective-permute-start(f32[88,704]{1,0:T(8,128)} %pad_maximum_fusion.5), channel_id=1, source_target_pairs={{0,96},{8,104},{16,112},{24,120},{32,0},{40,8},{48,16},{56,24},{64... | collective-permute-start | bytes 743432 | tf_op jit(solution)/shard_map/ppermute | solution.py:307
  231.2 27.6 %all-to-all-start.2 = ((f32[16,88,256]{2,1,0:T(8,128)}), f32[16,88,256]{2,1,0:T(8,128)S(1)}, u32[]{:S(2)}, u32[]{:S(2)}) async-start(f32[16,88,256]{2,1,0:T(8,128)} %query_grad.1), calls=%async_computation.2 | async-start | bytes 2883584 | tf_op jit(solution)/shard_map/all_to_all | solution.py:399
  263.1 19.3 %all-to-all-start.3 = ((f32[8,64,176]{2,1,0:T(8,128)}), f32[8,64,176]{2,1,0:T(8,128)S(1)}, u32[]{:S(2)}, u32[]{:S(2)}) async-start(f32[8,64,176]{2,1,0:T(8,128)} %latent_grad.1), calls=%async_computation.3 | async-start | bytes 1048576 | tf_op jit(solution)/shard_map/all_to_all | solution.py:406
  267.7 12.4 %collective-permute-start.7 = (f32[22,704]{1,0:T(8,128)S(1)}, f32[22,704]{1,0:T(8,128)S(1)}, u32[]{:S(2)}, u32[]{:S(2)}) collective-permute-start(f32[22,704]{1,0:T(8,128)S(1)} %get-tuple-element.65), channel_id=1, source_target_pairs={{0,1},{1,2},{2,3},{3,0},{4,5},{5,6},{6,7},{7,4},{8,9},{9,10},{10,1... | collective-permute-start | bytes 185864 | tf_op jit(solution)/shard_map/ppermute | solution.py:307
  269.8 10.9 %collective-permute-start.9 = (f32[22,704]{1,0:T(8,128)S(1)}, f32[22,704]{1,0:T(8,128)S(1)}, u32[]{:S(2)}, u32[]{:S(2)}) collective-permute-start(f32[22,704]{1,0:T(8,128)S(1)} %get-tuple-element.66), channel_id=1, source_target_pairs={{0,3},{1,0},{2,1},{3,2},{4,7},{5,4},{6,5},{7,6},{8,11},{9,8},{10,9... | collective-permute-start | bytes 185864 | tf_op jit(solution)/shard_map/ppermute | solution.py:307
  (27 other events, 215.7 us)
Sparse Core Ops, SparseCore 0:
  115.2 58.2 all-gather.2

commit v3 on v2

--- a/solution.py
+++ b/solution.py
@@ -134,7 +134,7 @@
 
 
 def backward_kernel(
-    chunk, q_ref, k_ref, v_ref, u_ref, lse_ref, delta_ref, dq_ref, dk_ref, dv_ref, done_ref
+    chunk, q_ref, k_ref, v_ref, u_ref, stat_ref, dq_ref, dkv_ref, done_ref
 ):
     head = pl.program_id(0)
     count = q_ref.shape[2]
@@ -144,48 +144,49 @@
     vals = v_ref[0].astype(F32).T.astype(BF16)
     key_grad = jnp.zeros(keys.shape, F32)
     value_grad = jnp.zeros(vals.shape, F32)
+    total = stat_ref[1, pl.ds(head, 1), :]
+    lse = stat_ref[0, pl.ds(head, 1), :] + jnp.log(total)
+    delta = stat_ref[2, pl.ds(head, 1), :] / total
     for start in range(0, count, chunk):
         cols = slice(start, start + chunk)
         q = q_ref[0, :, cols]
         u = u_ref[0, :, cols]
-        probs = jnp.exp(dot(keys, q) - lse_ref[pl.ds(head, 1), cols])
-        grad = (probs * (dot(vals, u) - delta_ref[pl.ds(head, 1), cols])).astype(BF16)
+        probs = jnp.exp(dot(keys, q) - lse[:, cols])
+        grad = (probs * (dot(vals, u) - delta[:, cols])).astype(BF16)
         value_grad += dot(probs.astype(BF16), u.astype(F32).T.astype(BF16))
         key_grad += dot(grad, q.astype(F32).T.astype(BF16))
         side, inner = divmod(start, half)
         dq_ref[side, 0, :, inner : inner + chunk] = dot(keys_t, grad)
-    dk_ref[0] = key_grad.T.astype(BF16)
-    dv_ref[0] = value_grad.T.astype(BF16)
+    dkv_ref[0, 0] = key_grad.T.astype(BF16)
+    dkv_ref[1, 0] = value_grad.T.astype(BF16)
     done_ref[...] = jnp.zeros_like(done_ref)
 
 
-def backward(q, k, v, u, lse, delta):
+def backward(q, k, v, u, stats):
     heads, _, count = q.shape
     tokens = k.shape[2]
     per_head = lambda n: pl.BlockSpec((1, HD, n), lambda h: (h, 0, 0))
-    whole = pl.BlockSpec((heads, count), lambda h: (0, 0))
     return pl.pallas_call(
         functools.partial(backward_kernel, min(256, count // 2)),
         grid=(heads,),
         in_specs=[
-            per_head(count), per_head(tokens), per_head(tokens), per_head(count), whole, whole,
+            per_head(count), per_head(tokens), per_head(tokens), per_head(count),
+            pl.BlockSpec((3, heads, count), lambda h: (0, 0, 0)),
         ],
         out_specs=[
             pl.BlockSpec((2, 1, HD, count // 2), lambda h: (0, h, 0, 0)),
-            per_head(tokens),
-            per_head(tokens),
+            pl.BlockSpec((2, 1, HD, tokens), lambda h: (0, h, 0, 0)),
             pl.BlockSpec((8, 128), lambda h: (0, 0)),
         ],
         out_shape=[
             jax.ShapeDtypeStruct((2, heads, HD, count // 2), F32),
-            jax.ShapeDtypeStruct((heads, HD, tokens), BF16),
-            jax.ShapeDtypeStruct((heads, HD, tokens), BF16),
+            jax.ShapeDtypeStruct((2, heads, HD, tokens), BF16),
             jax.ShapeDtypeStruct((8, 128), F32),
         ],
         compiler_params=params(),
         cost_estimate=cost(40 * heads * count * tokens * HD, 9e6),
         name="attend_back",
-    )(q, k, v, u, lse, delta)
+    )(q, k, v, u, stats)
 
 
 def sum_kernel(pieces_ref, after_ref, out_ref):
@@ -350,6 +351,7 @@
     side = 4
     share = width // seqs
     part = share // dps
+    padded = -(-part // 8) * 8
     rows = count // seqs
     upstream = cotangent[0]
     query_turned = query_weight.T
@@ -359,29 +361,24 @@
     )
     weighted, stats = forward(q, k, v, u)
 
-    top, total, delta = merge_stats(merge_stats(stats, side, True), side, False)
-    lse = top + jnp.log(total)
-    delta = delta / total
-    factor = (jnp.exp(stats[0] - top) / total).reshape(heads, 2, 1, half).transpose(1, 0, 2, 3)
+    whole = merge_stats(merge_stats(stats, side, True), side, False)
+    factor = (jnp.exp(stats[0] - whole[0]) / whole[1]).reshape(heads, 2, 1, half).transpose(1, 0, 2, 3)
 
     scaled = (weighted * factor).reshape(seqs, HD, half)
     attended_pieces = lax.all_to_all(scaled, "seq", 0, 0, tiled=True)
-    dq, dk, dv, done = backward(q, k, v, u, lse, delta)
+    dq, dkv, done = backward(q, k, v, u, whole)
+    seq, tp, done = lax.optimization_barrier((seq, tp, done))
 
     query_pieces = lax.all_to_all(dq.reshape(seqs, HD, half), "seq", 0, 0, tiled=True)
 
-    major, minor = seq // side, seq % side
-    cut = share // 16 * 8
-    along = lambda value, by: shift(value, "seq", by, side, True)
-    across = lambda value, by: shift(value, "seq", by, side, False)
-    key_term = dot(media_norm, dk.reshape(inner, -1), NT).reshape(side, side, share, inner)
-    value_term = dot(media_norm, dv.reshape(inner, -1), NT).reshape(side, side, share, inner)
-    key_rows = relay_sum(key_term.transpose(1, 0, 2, 3), minor, side // 2, along)
-    value_rows = relay_sum(value_term, major, side // 2, across)
-    key_rows = relay_sum(key_rows, major, cut, across)
-    value_rows = relay_sum(value_rows, minor, cut, along)
-    both = jnp.stack([key_rows, value_rows]).reshape(2, dps, part, inner).transpose(1, 0, 2, 3)
-    grad_key, grad_value = scatter_sum(both, "dp", dp)
+    blocks = media_norm.reshape(seqs, dps, part, -1).transpose(1, 0, 2, 3)
+    blocks = jnp.pad(blocks, ((0, 0), (0, 0), (0, padded - part), (0, 0)))
+    term = dot(blocks.reshape(dps * seqs * padded, -1), dkv.reshape(2 * inner, -1), NT)
+    term = term.reshape(dps, seqs * padded, 2 * inner)
+    term = relay_sum(term, dp, seqs * padded // 2, lambda value, by: shift(value, "dp", by))
+    term = lax.all_to_all(term.reshape(seqs, padded, 2 * inner), "seq", 0, 0, tiled=True)
+    term = jnp.sum(term, 0)[:part]
+    grad_key, grad_value = term[:, :inner], term[:, inner:]
 
     attended = lax.all_gather(sum_pieces(attended_pieces, done), "seq")
     cot_cols = lax.dynamic_slice_in_dim(upstream, seq * share, share, 1).T

time: 300 us -> 290 us (0.967)
  starting transfers between devices: 66.6 us -> 51.4 us
  waiting for transfers between devices: 86.4 us -> 95.9 us
  other arithmetic: 30.5 us -> 25 us
  local copies, waits for them, and re-layouts: 32 us -> 35.5 us
    ppermute x31 -> x16, waiting for transfers between devices: 70.1 us -> 32.8 us  [shift(): return lax.ppermute(value, axis, pairs)]
    ppermute x31 -> x16, starting transfers between devices: 48.1 us -> 26.8 us  [shift(): return lax.ppermute(value, axis, pairs)]
    all_to_all x0 -> x1, waiting for transfers between devices: none -> 19.3 us  [local(): lax.all_to_all(term.reshape(seqs, padded, 2 * inner), 'seq', 0, 0, tiled=...]
    all_to_all x1, waiting for transfers between devices: 7.49 us -> 23.6 us  [local(): attended_pieces = lax.all_to_all(scaled, 'seq', 0, 0, tiled=True)]
    all_to_all x1, waiting for transfers between devices: 0.01 us -> 13.8 us  [local(): lax.all_to_all(dq.reshape(seqs, HD, half), 'seq', 0, 0, tiled=True)]
    all_to_all x1, starting transfers between devices: 4.17 us -> 9.08 us  [local(): sent = lax.all_to_all(sent, 'seq', 0, 0, tiled=True)]
    all_to_all x0 -> x1, starting transfers between devices: none -> 3.72 us  [local(): lax.all_to_all(term.reshape(seqs, padded, 2 * inner), 'seq', 0, 0, tiled=...]
    add x4 -> x1, other arithmetic: 6.48 us -> 4.57 us  [relay_sum(): return pick(blocks, place) + send(ahead, 1) + send(behind, -1)]
  transfers between devices with their start and end apart: 37 -> 23, of which waited for: 21 -> 14; matrix products, arithmetic and copies ran while one was open for 17% -> 16% of each run, Pallas kernels for 11% -> 10%
where the time goes in v3:
time: 290 us; the launch traced here: 289 us
  waiting for transfers between devices  95.9 us (33%)
  Pallas kernels  63.5 us (22%)
  starting transfers between devices  51.4 us (18%)
  local copies, waits for them, and re-layouts  35.5 us (12%)
  other arithmetic  25 us (9%)
  between operations  14.4 us (5%)
    ppermute x16, waiting for transfers between devices, shift(): return lax.ppermute(value, axis, pairs)  32.8 us
    ppermute x16, starting transfers between devices, shift(): return lax.ppermute(value, axis, pairs)  26.8 us
    all_to_all x1, waiting for transfers between devices, local(): attended_pieces = lax.all_to_all(scaled, 'seq', 0, 0, tiled=True)  23.6 us
    all_to_all x1, waiting for transfers between devices, local(): lax.all_to_all(term.reshape(seqs, padded, 2 * inner), 'seq', 0, 0, tiled=...  19.3 us
    pallas_call x1, Pallas kernels, forward(): pl.pallas_call(functools.partial(forward_kernel, min(256, count // 2)), g...  16.8 us
    pallas_call x1, Pallas kernels, backward(): pl.pallas_call(functools.partial(backward_kernel, min(256, count // 2)),...  15.4 us
    pallas_call x1, Pallas kernels, project(): pl.pallas_call(project_kernel, grid=(steps,), in_specs=[rows(t), rows(c),...  14.9 us
    all_to_all x1, waiting for transfers between devices, local(): lax.all_to_all(dq.reshape(seqs, HD, half), 'seq', 0, 0, tiled=True)  13.8 us
  transfers between devices with their start and end apart: 23, of which 14 were waited for; matrix products, arithmetic and copies ran while one was open for 16% of the time, Pallas kernels for 10%

profile of v3, /device:TPU:0, one launch (start us, length us, event | category | flops | bytes accessed | tf_op | source)
XLA Modules:
  0.0 288.5 jit_solution(6181672548826280860)
XLA Ops:
  7.2 14.9 %project.1 = (bf16[1408,512]{1,0:T(8,128)(2,1)}, bf16[1408,1024]{1,0:T(8,128)(2,1)}, bf16[8,88,1024]{2,1,0:T(8,128)(2,1)}, bf16[8,88,512]{2,1,0:T(8,128)(2,1)}, ...) custom-call(bf16[512,1408]{1,0:T(8,128)(2,1)} %bitcast.128, bf16[1024,1408]{1,0:T(8,128)(2,1)} %latents_ref.1, ...), custom_call_target="tpu_custom_call" | custom-call | flops 6090129408 | bytes 24000000 | tf_op jit(solution)/shard_map/project/pallas_call | solution.py:74
  22.1 16.8 %attend.1 = (f32[2,8,88,512]{3,2,1,0:T(8,128)}, f32[3,8,1024]{2,1,0:T(8,128)}) custom-call(bf16[8,88,1024]{2,1,0:T(8,128)(2,1)} %get-tuple-element.23.q_ref, bf16[8,88,512]{2,1,0:T(8,128)(2,1)} %get-tuple-element.24.k_ref, bf16[8,88,512]{2,1,0:T(8,128)(2,1)} %get-tuple-element.25.v_ref, bf16[8,88,1024]{2,1,0:T(8,128)(2,1)} %get-tuple-element.26.u_ref), custom_call_target="tpu_custom_call" | custom-call | flops 5905580032 | bytes 9000000 | tf_op jit(solution)/shard_map/attend/pallas_call | solution.py:118
  38.8 2.8 collective-permute-start.2
  43.3 2.8 collective-permute-done.2
  51.4 4.1 %collective-permute-start.5 = (f32[3,8,1024]{2,1,0:T(8,128)S(1)}, f32[3,8,1024]{2,1,0:T(8,128)S(1)}, u32[]{:S(2)}, u32[]{:S(2)}) collective-permute-start(f32[3,8,1024]{2,1,0:T(8,128)S(1)} %pad_maximum_fusion.2), channel_id=1, source_target_pairs={{0,96},{8,104},{16,112},{24,120},{32,0},{40,8},{48,16},{56,24},{64... | collective-permute-start | bytes 294920 | tf_op jit(solution)/shard_map/ppermute | solution.py:308
  62.8 3.8 %broadcast_multiply_fusion = f32[2,8,88,512]{3,2,1,0:T(8,128)} fusion(f32[2,8,88,512]{3,2,1,0:T(8,128)} %get-tuple-element.30, f32[2,8,512]{2,1,0:T(8,128)S(1)} %divide_bitcast_fusion), kind=kLoop, calls=%fused_computation.7 | loop fusion | flops 720896 | bytes 5799936 | tf_op jit(solution)/shard_map/mul | solution.py:367
  66.6 3.7 %all-to-all-start = ((f32[16,88,512]{2,1,0:T(8,128)}), f32[16,88,512]{2,1,0:T(8,128)S(1)}, u32[]{:S(2)}, u32[]{:S(2)}) async-start(f32[16,88,512]{2,1,0:T(8,128)} %bitcast.101), calls=%async_computation | async-start | bytes 5767168 | tf_op jit(solution)/shard_map/all_to_all | solution.py:368
  71.2 15.4 %attend_back.1 = (f32[2,8,88,512]{3,2,1,0:T(8,128)}, bf16[2,8,88,512]{3,2,1,0:T(8,128)(2,1)}, f32[8,128]{1,0:T(8,128)}) custom-call(bf16[8,88,1024]{2,1,0:T(8,128)(2,1)} %get-tuple-element.23.q_ref, bf16[8,88,512]{2,1,0:T(8,128)(2,1)} %get-tuple-element.24.k_ref, bf16[8,88,512]{2,1,0:T(8,128)(2,1)} %get-tuple-element.25.v_ref, ...), custom_call_target="tpu_custom_call" | custom-call | flops 14763950080 | bytes 9000000 | tf_op jit(solution)/shard_map/attend_back/pallas_call | solution.py:169
  86.6 23.6 %all-to-all-done.pieces_ref = f32[16,88,512]{2,1,0:T(8,128)S(1)} async-done(((f32[16,88,512]{2,1,0:T(8,128)}), f32[16,88,512]{2,1,0:T(8,128)S(1)}, u32[]{:S(2)}, u32[]{:S(2)}) %all-to-all-start) | async-done | bytes 2883616 | tf_op jit(solution)/shard_map/all_to_all | solution.py:368
  129.0 3.7 %all-to-all-start.1 = ((f32[16,88,512]{2,1,0:T(8,128)}), f32[16,88,512]{2,1,0:T(8,128)S(1)}, u32[]{:S(2)}, u32[]{:S(2)}) async-start(f32[16,88,512]{2,1,0:T(8,128)} %bitcast.103), calls=%async_computation.1 | async-start | bytes 5767168 | tf_op jit(solution)/shard_map/all_to_all | solution.py:372
  132.7 17.5 %collective-permute-done.10 = f32[192,1408]{1,0:T(8,128)} collective-permute-done((f32[192,1408]{1,0:T(8,128)}, f32[192,1408]{1,0:T(8,128)}, u32[]{:S(2)}, u32[]{:S(2)}) %collective-permute-start.10) | collective-permute-done | bytes 1081376 | tf_op jit(solution)/shard_map/ppermute | solution.py:308
  161.2 13.8 %all-to-all-done.1.pieces_ref = f32[16,88,512]{2,1,0:T(8,128)S(1)} async-done(((f32[16,88,512]{2,1,0:T(8,128)}), f32[16,88,512]{2,1,0:T(8,128)S(1)}, u32[]{:S(2)}, u32[]{:S(2)}) %all-to-all-start.1) | async-done | bytes 2883616 | tf_op jit(solution)/shard_map/all_to_all | solution.py:372
  176.5 4.1 %query_grad.1 = f32[16,88,256]{2,1,0:T(8,128)} custom-call(f32[16,88,512]{2,1,0:T(8,128)} %copy-done, bf16[1408,512]{1,0:T(8,128)(2,1)} %constant_dynamic-slice_fusion.2.norm_ref), custom_call_target="tpu_custom_call" | custom-call | flops 126877696 | bytes 6000000 | tf_op jit(solution)/shard_map/query_grad/pallas_call | solution.py:269
  180.6 9.1 %all-to-all-start.2 = ((f32[16,88,256]{2,1,0:T(8,128)}), f32[16,88,256]{2,1,0:T(8,128)S(1)}, u32[]{:S(2)}, u32[]{:S(2)}) async-start(f32[16,88,256]{2,1,0:T(8,128)} %query_grad.1), calls=%async_computation.2 | async-start | bytes 2883584 | tf_op jit(solution)/shard_map/all_to_all | solution.py:396
  191.7 3.7 %constant_dynamic-slice_fusion.3 = (bf16[704,704]{1,0:T(8,128)(2,1)}, bf16[704,704]{1,0:T(8,128)(2,1)S(1)}) fusion(bf16[704,1408]{1,0:T(8,128)(2,1)} %ow_ref.1, s32[]{:T(128)S(6)} %select_n.75, s32[]{:T(128)S(6)} %select_n.73), kind=kLoop, calls=%fused_computation.62 | loop fusion | bytes 3964936 | tf_op jit(solution)/shard_map/dynamic_slice | solution.py:386
  202.6 6.4 %all-to-all-done.2 = f32[16,88,256]{2,1,0:T(8,128)S(1)} async-done(((f32[16,88,256]{2,1,0:T(8,128)}), f32[16,88,256]{2,1,0:T(8,128)S(1)}, u32[]{:S(2)}, u32[]{:S(2)}) %all-to-all-start.2) | async-done | bytes 1441824 | tf_op jit(solution)/shard_map/all_to_all | solution.py:396
  209.8 3.2 %latent_grad.1 = f32[8,64,176]{2,1,0:T(8,128)} custom-call(f32[8,88,64]{2,1,0:T(8,128)} %constant_dynamic-slice_fusion.1.pieces_ref, bf16[704,1408]{1,0:T(8,128)(2,1)} %bitcast.105, bf16[64,1408]{1,0:T(8,128)(2,1)} %constant_dynamic-slice_fusion.latents_ref, bf16[64,1408]{1,0:T(8,128)(2,1)} %dynamic-slice_bitcast_fusion.6.cot_ref), custom_call_target="tpu_custom_call" | custom-call | flops 126877696 | bytes 4000000 | tf_op jit(solution)/shard_map/latent_grad/pallas_call | solution.py:291
  213.0 3.7 %all-to-all-start.3 = ((f32[8,64,176]{2,1,0:T(8,128)}), f32[8,64,176]{2,1,0:T(8,128)S(1)}, u32[]{:S(2)}, u32[]{:S(2)}) async-start(f32[8,64,176]{2,1,0:T(8,128)} %latent_grad.1), calls=%async_computation.3 | async-start | bytes 1048576 | tf_op jit(solution)/shard_map/all_to_all | solution.py:403
  216.8 6.5 %project_out.1 = (f32[88,704]{1,0:T(8,128)}, f32[704,1024]{1,0:T(8,128)}, f32[704,1024]{1,0:T(8,128)}) custom-call(f32[2,8,88,512]{3,2,1,0:T(8,128)} %bitcast.125, bf16[88,1024]{1,0:T(8,128)(2,1)} %bitcast.109, bf16[704,704]{1,0:T(8,128)(2,1)} %bitcast.108, bf16[704,704]{1,0:T(8,128)(2,1)} %bitcast.107), custom_call_target="tpu_custom_call" | custom-call | flops 2030043136 | bytes 12000000 | tf_op jit(solution)/shard_map/project_out/pallas_call | solution.py:227
  223.7 4.6 %fusion.1 = f32[384,1408]{1,0:T(8,128)} fusion(f32[384,1408]{1,0:T(8,128)} %collective-permute-done.13, f32[384,1408]{1,0:T(8,128)} %collective-permute-done.11, f32[4,384,1408]{2,1,0:T(8,128)} %copy-done.2, s32[]{:T(128)S(6)} %select_n.80), kind=kLoop, calls=%fused_computation.5 | loop fusion | flops 1081344 | bytes 8650756 | tf_op jit(solution)/shard_map/add | solution.py:331
  228.3 3.7 %all-to-all-start.4 = ((f32[16,24,1408]{2,1,0:T(8,128)}), f32[16,24,1408]{2,1,0:T(8,128)S(1)}, u32[]{:S(2)}, u32[]{:S(2)}) async-start(f32[16,24,1408]{2,1,0:T(8,128)} %bitcast.48), calls=%async_computation.4 | async-start | bytes 4325376 | tf_op jit(solution)/shard_map/all_to_all | solution.py:379
  239.3 3.4 %constant_dynamic-slice_fusion.6 = bf16[1024,704]{1,0:T(8,128)(2,1)} fusion(bf16[1024,1408]{1,0:T(8,128)(2,1)} %latents_ref.1, s32[]{:T(128)S(6)} %select_n.73), kind=kLoop, calls=%fused_computation.65 | loop fusion | bytes 2883588 | tf_op jit(solution)/shard_map/dynamic_slice | solution.py:387
  247.5 19.3 %all-to-all-done.4 = f32[16,24,1408]{2,1,0:T(8,128)S(1)} async-done(((f32[16,24,1408]{2,1,0:T(8,128)}), f32[16,24,1408]{2,1,0:T(8,128)S(1)}, u32[]{:S(2)}, u32[]{:S(2)}) %all-to-all-start.4) | async-done | bytes 2162720 | tf_op jit(solution)/shard_map/all_to_all | solution.py:379
  277.0 4.6 %fusion.2 = bf16[1,1024,704]{1,2,0:T(8,128)(2,1)} fusion(f32[704,1024]{1,0:T(8,128)} %get-tuple-element.33, f32[704,1024]{1,0:T(8,128)} %collective-permute-done.6, bf16[1024,704]{0,1:T(8,128)(2,1)S(1)} %copy-done.3), kind=kLoop, calls=%fused_computation.6 | loop fusion | flops 2883584 | bytes 8650752 | tf_op jit(solution)/shard_map/broadcast_in_dim | solution.py:390
  (90 shorter events, 78.8 us)
Async XLA Ops:
  38.8 7.3 %collective-permute-start.2 = (f32[3,8,1024]{2,1,0:T(8,128)}, f32[3,8,1024]{2,1,0:T(8,128)S(1)}, u32[]{:S(2)}, u32[]{:S(2)}) collective-permute-start(f32[3,8,1024]{2,1,0:T(8,128)} %get-tuple-element.27), channel_id=1, source_target_pairs={{0,24},{8,0},{16,8},{24,16},{32,56},{40,32},{48,40},{56,48},{64,88... | collective-permute-start | bytes 294920 | tf_op jit(solution)/shard_map/ppermute | solution.py:308
  41.7 7.1 %collective-permute-start.1 = (f32[3,8,1024]{2,1,0:T(8,128)}, f32[3,8,1024]{2,1,0:T(8,128)S(1)}, u32[]{:S(2)}, u32[]{:S(2)}) collective-permute-start(f32[3,8,1024]{2,1,0:T(8,128)} %get-tuple-element.27), channel_id=1, source_target_pairs={{0,16},{8,24},{16,0},{24,8},{32,48},{40,56},{48,32},{56,40},{64,80... | collective-permute-start | bytes 294920 | tf_op jit(solution)/shard_map/ppermute | solution.py:308
  42.5 7.3 %collective-permute-start = (f32[3,8,1024]{2,1,0:T(8,128)}, f32[3,8,1024]{2,1,0:T(8,128)S(1)}, u32[]{:S(2)}, u32[]{:S(2)}) collective-permute-start(f32[3,8,1024]{2,1,0:T(8,128)} %get-tuple-element.27), channel_id=1, source_target_pairs={{0,8},{8,16},{16,24},{24,0},{32,40},{40,48},{48,56},{56,32},{64,72... | collective-permute-start | bytes 294920 | tf_op jit(solution)/shard_map/ppermute | solution.py:308
  51.4 7.9 %collective-permute-start.5 = (f32[3,8,1024]{2,1,0:T(8,128)S(1)}, f32[3,8,1024]{2,1,0:T(8,128)S(1)}, u32[]{:S(2)}, u32[]{:S(2)}) collective-permute-start(f32[3,8,1024]{2,1,0:T(8,128)S(1)} %pad_maximum_fusion.2), channel_id=1, source_target_pairs={{0,96},{8,104},{16,112},{24,120},{32,0},{40,8},{48,16},{56,24},{64... | collective-permute-start | bytes 294920 | tf_op jit(solution)/shard_map/ppermute | solution.py:308
  55.5 6.5 %collective-permute-start.4 = (f32[3,8,1024]{2,1,0:T(8,128)S(1)}, f32[3,8,1024]{2,1,0:T(8,128)S(1)}, u32[]{:S(2)}, u32[]{:S(2)}) collective-permute-start(f32[3,8,1024]{2,1,0:T(8,128)S(1)} %pad_maximum_fusion.2), channel_id=1, source_target_pairs={{0,64},{8,72},{16,80},{24,88},{32,96},{40,104},{48,112},{56,120},{... | collective-permute-start | bytes 294920 | tf_op jit(solution)/shard_map/ppermute | solution.py:308
  55.5 7.2 %collective-permute-start.3 = (f32[3,8,1024]{2,1,0:T(8,128)S(1)}, f32[3,8,1024]{2,1,0:T(8,128)S(1)}, u32[]{:S(2)}, u32[]{:S(2)}) collective-permute-start(f32[3,8,1024]{2,1,0:T(8,128)S(1)} %pad_maximum_fusion.2), channel_id=1, source_target_pairs={{0,32},{8,40},{16,48},{24,56},{32,64},{40,72},{48,80},{56,88},{64,... | collective-permute-start | bytes 294920 | tf_op jit(solution)/shard_map/ppermute | solution.py:308
  66.6 43.6 %all-to-all-start = ((f32[16,88,512]{2,1,0:T(8,128)}), f32[16,88,512]{2,1,0:T(8,128)S(1)}, u32[]{:S(2)}, u32[]{:S(2)}) async-start(f32[16,88,512]{2,1,0:T(8,128)} %bitcast.101), calls=%async_computation | async-start | bytes 5767168 | tf_op jit(solution)/shard_map/all_to_all | solution.py:368
  70.3 146.5 %all-gather.3.cloned.1.call-start = ((), (), s32[]{:S(2)}) async-start(), calls=%async_computation.5 | async-start | bytes 3063808 | tf_op jit(solution)/shard_map/all_gather | solution.py:383
  125.7 24.4 %collective-permute-start.10 = (f32[192,1408]{1,0:T(8,128)}, f32[192,1408]{1,0:T(8,128)}, u32[]{:S(2)}, u32[]{:S(2)}) collective-permute-start(f32[192,1408]{1,0:T(8,128)} %get-tuple-element.44), channel_id=1, source_target_pairs={{0,1},{1,2},{2,3},{3,0},{4,5},{5,6},{6,7},{7,4},{8,9},{9,10},{10,1... | collective-permute-start | bytes 3244040 | tf_op jit(solution)/shard_map/ppermute | solution.py:308
  127.4 23.0 %collective-permute-start.12 = (f32[192,1408]{1,0:T(8,128)}, f32[192,1408]{1,0:T(8,128)}, u32[]{:S(2)}, u32[]{:S(2)}) collective-permute-start(f32[192,1408]{1,0:T(8,128)} %get-tuple-element.46), channel_id=1, source_target_pairs={{0,3},{1,0},{2,1},{3,2},{4,7},{5,4},{6,5},{7,6},{8,11},{9,8},{10,9... | collective-permute-start | bytes 3244040 | tf_op jit(solution)/shard_map/ppermute | solution.py:308
  129.0 46.0 %all-to-all-start.1 = ((f32[16,88,512]{2,1,0:T(8,128)}), f32[16,88,512]{2,1,0:T(8,128)S(1)}, u32[]{:S(2)}, u32[]{:S(2)}) async-start(f32[16,88,512]{2,1,0:T(8,128)} %bitcast.103), calls=%async_computation.1 | async-start | bytes 5767168 | tf_op jit(solution)/shard_map/all_to_all | solution.py:372
  154.3 69.4 %collective-permute-start.13 = (f32[384,1408]{1,0:T(8,128)}, f32[384,1408]{1,0:T(8,128)}, u32[]{:S(2)}, u32[]{:S(2)}) collective-permute-start(f32[384,1408]{1,0:T(8,128)} %pad_maximum_fusion.1), channel_id=1, source_target_pairs={{0,3},{1,0},{2,1},{3,2},{4,7},{5,4},{6,5},{7,6},{8,11},{9,8},{10,9... | collective-permute-start | bytes 6488072 | tf_op jit(solution)/shard_map/ppermute | solution.py:308
  158.6 65.1 %collective-permute-start.11 = (f32[384,1408]{1,0:T(8,128)}, f32[384,1408]{1,0:T(8,128)}, u32[]{:S(2)}, u32[]{:S(2)}) collective-permute-start(f32[384,1408]{1,0:T(8,128)} %pad_maximum_fusion), channel_id=1, source_target_pairs={{0,1},{1,2},{2,3},{3,0},{4,5},{5,6},{6,7},{7,4},{8,9},{9,10},{10,1... | collective-permute-start | bytes 6488072 | tf_op jit(solution)/shard_map/ppermute | solution.py:308
  180.6 28.4 %all-to-all-start.2 = ((f32[16,88,256]{2,1,0:T(8,128)}), f32[16,88,256]{2,1,0:T(8,128)S(1)}, u32[]{:S(2)}, u32[]{:S(2)}) async-start(f32[16,88,256]{2,1,0:T(8,128)} %query_grad.1), calls=%async_computation.2 | async-start | bytes 2883584 | tf_op jit(solution)/shard_map/all_to_all | solution.py:396
  213.0 15.2 %all-to-all-start.3 = ((f32[8,64,176]{2,1,0:T(8,128)}), f32[8,64,176]{2,1,0:T(8,128)S(1)}, u32[]{:S(2)}, u32[]{:S(2)}) async-start(f32[8,64,176]{2,1,0:T(8,128)} %latent_grad.1), calls=%async_computation.3 | async-start | bytes 1048576 | tf_op jit(solution)/shard_map/all_to_all | solution.py:403
  223.3 53.7 %collective-permute-start.6 = (f32[704,1024]{1,0:T(8,128)}, f32[704,1024]{1,0:T(8,128)}, u32[]{:S(2)}, u32[]{:S(2)}) collective-permute-start(f32[704,1024]{1,0:T(8,128)} %get-tuple-element.34), channel_id=1, source_target_pairs={{0,4},{4,0},{1,5},{5,1},{2,6},{6,2},{3,7},{7,3},{8,12},{12,8},{9,1... | collective-permute-start | bytes 8650760 | tf_op jit(solution)/shard_map/ppermute | solution.py:389
  228.3 38.5 %all-to-all-start.4 = ((f32[16,24,1408]{2,1,0:T(8,128)}), f32[16,24,1408]{2,1,0:T(8,128)S(1)}, u32[]{:S(2)}, u32[]{:S(2)}) async-start(f32[16,24,1408]{2,1,0:T(8,128)} %bitcast.48), calls=%async_computation.4 | async-start | bytes 4325376 | tf_op jit(solution)/shard_map/all_to_all | solution.py:379
  234.1 11.1 %collective-permute-start.7 = (f32[22,704]{1,0:T(8,128)}, f32[22,704]{1,0:T(8,128)S(1)}, u32[]{:S(2)}, u32[]{:S(2)}) collective-permute-start(f32[22,704]{1,0:T(8,128)} %get-tuple-element.56), channel_id=1, source_target_pairs={{0,1},{1,2},{2,3},{3,0},{4,5},{5,6},{6,7},{7,4},{8,9},{9,10},{10,1... | collective-permute-start | bytes 185864 | tf_op jit(solution)/shard_map/ppermute | solution.py:308
  235.8 9.4 %collective-permute-start.9 = (f32[22,704]{1,0:T(8,128)}, f32[22,704]{1,0:T(8,128)S(1)}, u32[]{:S(2)}, u32[]{:S(2)}) collective-permute-start(f32[22,704]{1,0:T(8,128)} %get-tuple-element.57), channel_id=1, source_target_pairs={{0,3},{1,0},{2,1},{3,2},{4,7},{5,4},{6,5},{7,6},{8,11},{9,8},{10,9... | collective-permute-start | bytes 185864 | tf_op jit(solution)/shard_map/ppermute | solution.py:308
  237.3 7.9 %collective-permute-start.8 = (f32[22,704]{1,0:T(8,128)S(1)}, f32[22,704]{1,0:T(8,128)}, u32[]{:S(2)}, u32[]{:S(2)}) collective-permute-start(f32[22,704]{1,0:T(8,128)S(1)} %get-tuple-element.58), channel_id=1, source_target_pairs={{0,2},{1,3},{2,0},{3,1},{4,6},{5,7},{6,4},{7,5},{8,10},{9,11},{10,... | collective-permute-start | bytes 185864 | tf_op jit(solution)/shard_map/ppermute | solution.py:308
  245.2 21.7 %copy-start.7 = (f32[88,704]{1,0:T(8,128)S(1)}, f32[88,704]{1,0:T(8,128)}, u32[]{:S(2)}) copy-start(f32[88,704]{1,0:T(8,128)} %get-tuple-element.39) | copy-start | bytes 743428
  267.0 6.4 %collective-permute-start.14 = (f32[22,704]{1,0:T(8,128)S(1)}, f32[22,704]{1,0:T(8,128)S(1)}, u32[]{:S(2)}, u32[]{:S(2)}) collective-permute-start(f32[22,704]{1,0:T(8,128)S(1)} %get-tuple-element.53), channel_id=1, source_target_pairs={{0,1},{1,2},{2,3},{3,0},{4,5},{5,6},{6,7},{7,4},{8,9},{9,10},{10,1... | collective-permute-start | bytes 185864 | tf_op jit(solution)/shard_map/ppermute | solution.py:308
  269.2 5.1 %collective-permute-start.16 = (f32[22,704]{1,0:T(8,128)S(1)}, f32[22,704]{1,0:T(8,128)S(1)}, u32[]{:S(2)}, u32[]{:S(2)}) collective-permute-start(f32[22,704]{1,0:T(8,128)S(1)} %get-tuple-element.54), channel_id=1, source_target_pairs={{0,3},{1,0},{2,1},{3,2},{4,7},{5,4},{6,5},{7,6},{8,11},{9,8},{10,9... | collective-permute-start | bytes 185864 | tf_op jit(solution)/shard_map/ppermute | solution.py:308
  270.5 5.9 %collective-permute-start.15 = (f32[22,704]{1,0:T(8,128)S(1)}, f32[22,704]{1,0:T(8,128)S(1)}, u32[]{:S(2)}, u32[]{:S(2)}) collective-permute-start(f32[22,704]{1,0:T(8,128)S(1)} %get-tuple-element.55), channel_id=1, source_target_pairs={{0,2},{1,3},{2,0},{3,1},{4,6},{5,7},{6,4},{7,5},{8,10},{9,11},{10,... | collective-permute-start | bytes 185864 | tf_op jit(solution)/shard_map/ppermute | solution.py:308
  (8 other events, 47.8 us)
Sparse Core Ops, SparseCore 0:
  114.5 66.8 all-gather.2
